TPU v7x, 256 devices: a whole 4x4x8 slice. The times are simulated.
256 devices in a mesh: rep: 4 (over x_hi, core), lat: 8 (over x_lo, y), lon: 8 (over z).
Axes of the slice: x: 4 (x_hi: 2, x_lo: 2; x = x_hi * 2 + x_lo), y: 4, z: 8, core: 2. Of those that a mesh axis runs over, the one named last changes fastest.
Arguments:
- tokens: bfloat16 [4, 8, 48, 96, 192], P('rep', None, 'lat', 'lon'), may hold values from -6 to 6
- cotangent: bfloat16 [4, 8, 48, 96, 192], P('rep', None, 'lat', 'lon'), may hold values from -6 to 6
- gain_a: float32 [192], replicated, may hold values from 0.1 to 1.9
- qkv_a: bfloat16 [192, 576], replicated, may hold values from -0.4375 to 0.4375
- out_a: bfloat16 [192, 192], replicated, may hold values from -0.4375 to 0.4375
- bias_a: float32 [6, 144, 144], replicated, may hold values from -6 to 330
- gain_b: float32 [192], replicated, may hold values from 0.1 to 1.9
- qkv_b: bfloat16 [192, 576], replicated, may hold values from -0.4375 to 0.4375
- out_b: bfloat16 [192, 192], replicated, may hold values from -0.4375 to 0.4375
- bias_b: float32 [6, 144, 144], replicated, may hold values from -6 to 330
Outputs:
- d_tokens: bfloat16 [4, 8, 48, 96, 192], P('rep', None, 'lat', 'lon')
- gain_grad_a: float32 [192], replicated
- qkv_grad_a: float32 [192, 576], replicated
- out_grad_a: float32 [192, 192], replicated
- bias_grad_a: float32 [6, 144, 144], replicated
- gain_grad_b: float32 [192], replicated
- qkv_grad_b: float32 [192, 576], replicated
- out_grad_b: float32 [192, 192], replicated
- bias_grad_b: float32 [6, 144, 144], replicated
All inputs are finite; a program needn't handle non-finite values.
Results may differ from a plain program's by a relative error of at most 0.028.
Values may be sent and summed in bfloat16 or wider, within the bound.
A program may use at most 64 MiB of HBM per device.

v0:
```python
import jax
import jax.numpy as jnp
from jax import lax
from jax.sharding import PartitionSpec as P

WZ = 2
WLAT = 6
WLON = 12


def from_behind(value, axis, steps):
    count = lax.axis_size(axis)
    pairs = [(source, (source + steps) % count) for source in range(count)]
    return lax.ppermute(value, axis, pairs)


def to_windows(grid, wz, wl, wo):
    b, z, l, o, c = grid.shape
    boxed = grid.reshape(b, z // wz, wz, l // wl, wl, o // wo, wo, c)
    boxed = boxed.transpose(0, 1, 3, 5, 2, 4, 6, 7)
    return boxed.reshape(-1, wz * wl * wo, c)


def from_windows(windows_in, full_shape, wz, wl, wo):
    b, z, l, o, c = full_shape
    boxed = windows_in.reshape(b, z // wz, l // wl, o // wo, wz, wl, wo, c)
    boxed = boxed.transpose(0, 1, 4, 2, 5, 3, 6, 7)
    return boxed.reshape(b, z, l, o, c)


def inner_rows(left, right):
    return lax.dot_general(
        left, right, (((0,), (0,)), ((), ())), preferred_element_type=jnp.float32
    )


def attend_forward(block_in, labels, gain, w_qkv, w_out, bias):
    count, window_len, width = block_in.shape
    heads = bias.shape[0]
    head_width = width // heads
    factor = head_width ** (-0.5)
    flat = block_in.reshape(-1, width).astype(jnp.float32)
    center = flat - jnp.mean(flat, axis=-1, keepdims=True)
    inv_std = lax.rsqrt(jnp.mean(center * center, axis=-1, keepdims=True) + 1e-05)
    unit = center * inv_std
    normed = (unit * gain).astype(jnp.bfloat16)
    qkv = jnp.dot(normed, w_qkv, preferred_element_type=jnp.float32).astype(jnp.bfloat16)
    qkv = qkv.reshape(count, window_len, 3, heads, head_width).transpose(2, 0, 3, 1, 4)
    query, key, value = (qkv[0], qkv[1], qkv[2])
    scores = (
        jnp.einsum("nhad,nhbd->nhab", query, key, preferred_element_type=jnp.float32) * factor
        + bias
    )
    if labels is not None:
        allowed = labels[:, None, :, None] == labels[:, None, None, :]
        scores = jnp.where(allowed, scores, -1e30)
    probs = jax.nn.softmax(scores, axis=-1)
    probs_bf = probs.astype(jnp.bfloat16)
    attended = jnp.einsum(
        "nhab,nhbd->nhad", probs_bf, value, preferred_element_type=jnp.float32
    ).astype(jnp.bfloat16)
    attended = attended.transpose(0, 2, 1, 3).reshape(-1, width)
    mixed = jnp.dot(attended, w_out, preferred_element_type=jnp.float32)
    block_out = (flat + mixed).astype(jnp.bfloat16).reshape(count, window_len, width)
    return (block_out, (unit, inv_std, normed, query, key, value, probs, probs_bf, attended))


def attend_backward(cache, incoming, gain, w_qkv, w_out):
    unit, inv_std, normed, query, key, value, probs, probs_bf, attended = cache
    count, heads, window_len, head_width = query.shape
    width = heads * head_width
    factor = head_width ** (-0.5)
    flat_in = incoming.reshape(-1, width)
    out_grad = inner_rows(attended, flat_in)
    d_attended = lax.dot_general(
        flat_in, w_out, (((1,), (1,)), ((), ())), preferred_element_type=jnp.float32
    ).astype(jnp.bfloat16)
    d_attended = d_attended.reshape(count, window_len, heads, head_width).transpose(0, 2, 1, 3)
    d_probs = jnp.einsum("nhad,nhbd->nhab", d_attended, value, preferred_element_type=jnp.float32)
    d_value = jnp.einsum(
        "nhab,nhad->nhbd", probs_bf, d_attended, preferred_element_type=jnp.float32
    ).astype(jnp.bfloat16)
    d_scores = probs * (d_probs - jnp.sum(probs * d_probs, axis=-1, keepdims=True))
    bias_grad = jnp.sum(d_scores, axis=0)
    d_scaled = (d_scores * factor).astype(jnp.bfloat16)
    d_query = jnp.einsum(
        "nhab,nhbd->nhad", d_scaled, key, preferred_element_type=jnp.float32
    ).astype(jnp.bfloat16)
    d_key = jnp.einsum(
        "nhab,nhad->nhbd", d_scaled, query, preferred_element_type=jnp.float32
    ).astype(jnp.bfloat16)
    d_qkv = (
        jnp.stack([d_query, d_key, d_value], axis=0).transpose(1, 3, 0, 2, 4).reshape(-1, 3 * width)
    )
    qkv_grad = inner_rows(normed, d_qkv)
    d_normed = lax.dot_general(
        d_qkv, w_qkv, (((1,), (1,)), ((), ())), preferred_element_type=jnp.float32
    )
    gain_grad = jnp.sum(d_normed * unit, axis=0)
    d_hat = d_normed * gain
    d_input = flat_in.astype(jnp.float32) + inv_std * (
        d_hat
        - jnp.mean(d_hat, axis=-1, keepdims=True)
        - unit * jnp.mean(d_hat * unit, axis=-1, keepdims=True)
    )
    return (d_input.reshape(count, window_len, width), (gain_grad, qkv_grad, out_grad, bias_grad))


def local(tokens, cotangent, gain_a, qkv_a, out_a, bias_a, gain_b, qkv_b, out_b, bias_b):
    full_shape = tokens.shape
    levels, lat_dev, lon_dev = (full_shape[1], full_shape[2], full_shape[3])
    half_z, half_lat, half_lon = (WZ // 2, WLAT // 2, WLON // 2)
    windows_in = to_windows(tokens, WZ, WLAT, WLON)
    middle_windows, cache_a = attend_forward(windows_in, None, gain_a, qkv_a, out_a, bias_a)
    middle = from_windows(middle_windows, full_shape, WZ, WLAT, WLON)
    rows_mid, rows_cot = from_behind(
        (middle[:, :, :half_lat], cotangent[:, :, :half_lat]), "lat", -1
    )
    middle = jnp.concatenate([middle[:, :, half_lat:], rows_mid], axis=2)
    upstream = jnp.concatenate([cotangent[:, :, half_lat:], rows_cot], axis=2)
    cols_mid, cols_cot = from_behind(
        (middle[:, :, :, :half_lon], upstream[:, :, :, :half_lon]), "lon", -1
    )
    middle = jnp.roll(
        jnp.concatenate([middle[:, :, :, half_lon:], cols_mid], axis=3), -half_z, axis=1
    )
    upstream = jnp.roll(
        jnp.concatenate([upstream[:, :, :, half_lon:], cols_cot], axis=3), -half_z, axis=1
    )
    level_index = lax.broadcasted_iota(jnp.int32, (1, levels, lat_dev, lon_dev, 1), 1)
    row_index = (
        lax.broadcasted_iota(jnp.int32, (1, levels, lat_dev, lon_dev, 1), 2)
        + lax.axis_index("lat") * lat_dev
    )
    total_rows = lat_dev * lax.axis_size("lat")
    labels = 2 * (level_index >= levels - half_z).astype(jnp.int32) + (
        row_index >= total_rows - half_lat
    ).astype(jnp.int32)
    label_windows = to_windows(labels, WZ, WLAT, WLON)[..., 0]
    cache_b = attend_forward(
        to_windows(middle, WZ, WLAT, WLON), label_windows, gain_b, qkv_b, out_b, bias_b
    )[1]
    d_shifted, grads_b = attend_backward(
        cache_b, to_windows(upstream, WZ, WLAT, WLON), gain_b, qkv_b, out_b
    )
    d_rolled = jnp.roll(
        from_windows(d_shifted.astype(jnp.bfloat16), full_shape, WZ, WLAT, WLON), half_z, axis=1
    )
    back_cols = from_behind(d_rolled[:, :, :, lon_dev - half_lon :], "lon", 1)
    d_rolled = jnp.concatenate([back_cols, d_rolled[:, :, :, : lon_dev - half_lon]], axis=3)
    back_rows = from_behind(d_rolled[:, :, lat_dev - half_lat :], "lat", 1)
    d_middle = jnp.concatenate([back_rows, d_rolled[:, :, : lat_dev - half_lat]], axis=2)
    d_regular, grads_a = attend_backward(
        cache_a, to_windows(d_middle, WZ, WLAT, WLON), gain_a, qkv_a, out_a
    )
    summed = lax.psum(
        (
            grads_a[0],
            grads_a[1],
            grads_a[2],
            grads_a[3],
            grads_b[0],
            grads_b[1],
            grads_b[2],
            grads_b[3],
        ),
        ("rep", "lat", "lon"),
    )
    grads_a = summed[:4]
    grads_b = summed[4:]
    d_tokens = from_windows(d_regular.astype(jnp.bfloat16), full_shape, WZ, WLAT, WLON)
    return (
        d_tokens,
        grads_a[0],
        grads_a[1],
        grads_a[2],
        grads_a[3],
        grads_b[0],
        grads_b[1],
        grads_b[2],
        grads_b[3],
    )


def solution(mesh):
    placed = (
        P("rep", None, "lat", "lon", None),
        P("rep", None, "lat", "lon", None),
        P(),
        P(),
        P(),
        P(),
        P(),
        P(),
        P(),
        P(),
    )
    return jax.shard_map(
        local,
        mesh=mesh,
        in_specs=placed,
        out_specs=(P("rep", None, "lat", "lon", None), P(), P(), P(), P(), P(), P(), P(), P()),
        check_vma=False,
    )
```

profile of v0, /device:TPU:1, one launch (start us, length us, event | category | flops | bytes accessed | tf_op | source)
XLA Modules:
  0.0 418.3 jit_solution(9248893363767012842)
XLA Ops:
  7.3 1.8 fusion.90
  9.0 4.5 %collective-permute-start = (bf16[1,8,3,12,192]{4,1,3,2,0:T(8,128)(2,1)}, bf16[1,8,3,12,192]{4,1,3,2,0:T(8,128)(2,1)}, u32[]{:S(2)}, u32[]{:S(2)}) collective-permute-start(bf16[1,8,3,12,192]{4,1,3,2,0:T(8,128)(2,1)} %get-tuple-element.79), channel_id=1, source_target_pairs={{0,56},{8,0},{16,8},{24,16},{32,24},{40,32},{48,40},{56,48},{1,57}... | collective-permute-start | bytes 331784 | tf_op jit(solution)/shard_map/ppermute | solution.py:14
  16.1 1.2 multiply_reduce_fusion.3
  19.5 3.1 reshape.361
  22.8 2.0 copy.165
  25.6 1.4 fusion.91
  27.4 1.3 copy-done.4
  33.4 1.4 copy.178
  35.5 5.6 %collective-permute-start.3 = (bf16[1,8,6,6,192]{4,3,2,1,0:T(8,128)(2,1)S(1)}, bf16[1,8,6,6,192]{4,3,2,1,0:T(8,128)(2,1)S(1)}, u32[]{:S(2)}, u32[]{:S(2)}) collective-permute-start(bf16[1,8,6,6,192]{4,3,2,1,0:T(8,128)(2,1)S(1)} %get-tuple-element.73), channel_id=1, source_target_pairs={{0,7},{1,0},{2,1},{3,2},{4,3},{5,4},{6,5},{7,6},{8,15},{9,8},{10,9... | collective-permute-start | bytes 331784 | tf_op jit(solution)/shard_map/ppermute | solution.py:14
  44.7 1.9 collective-permute-done.1
  52.3 1.2 copy.232
  53.6 4.8 %fusion.92 = (f32[4,6,144]{2,1,0:T(8,128)S(1)}, f32[4,6,144,144]{2,3,1,0:T(8,128)}) fusion(f32[6,144,144]{1,2,0:T(8,128)} %copy.178, pred[4,144,144]{1,2,0:T(8,128)(4,1)} %broadcast_compare_fusion, bf16[3,4,6,144,32]{3,4,2,1,0:T(8,128)(2,1)} %bitcast.111), kind=kOutput, calls=%fused_computation.150 | convolution fusion | flops 34338960 | bytes 3823104 | tf_op jit(solution)/shard_map/sub | solution.py:57
  58.4 3.3 fusion.25
  62.4 2.5 fusion.39
  64.9 6.4 %fusion.18 = bf16[1,4,6,144,32]{3,4,2,1,0:T(8,128)(2,1)S(1)} fusion(bf16[3,4,6,144,32]{3,4,2,1,0:T(8,128)(2,1)S(1)} %bitcast.114, f32[4,6,144,144]{2,3,1,0:T(8,128)} %fusion.39, f32[4,6,144,144]{2,3,1,0:T(8,128)} %get-tuple-element.83, f32[4,6,144]{2,1,0:T(8,128)} %copy-done.29), kind=kOutput, calls=%fused_computation.37 | convolution fusion | flops 35448336 | bytes 14835712 | tf_op jit(solution)/shard_map/nhab,nhad->nhbd/dot_general | solution.py:89
  71.4 7.3 %fusion.23 = bf16[1,4,6,144,32]{3,4,2,1,0:T(8,128)(2,1)} fusion(bf16[3,4,6,144,32]{3,4,2,1,0:T(8,128)(2,1)S(1)} %bitcast.115, f32[4,6,144,144]{2,3,1,0:T(8,128)} %fusion.39, f32[4,6,144,144]{2,3,1,0:T(8,128)} %get-tuple-element.83, f32[4,6,144]{2,1,0:T(8,128)} %copy-done.29), kind=kOutput, calls=%fused_computation.42 | convolution fusion | flops 35448336 | bytes 14835712 | tf_op jit(solution)/shard_map/nhab,nhbd->nhad/dot_general | solution.py:86
  78.7 7.3 %fusion.94 = f32[6,144,144]{1,2,0:T(8,128)} fusion(f32[4,6,144,144]{2,3,1,0:T(8,128)} %fusion.39, f32[4,6,144,144]{2,3,1,0:T(8,128)} %get-tuple-element.83, f32[4,6,144]{2,1,0:T(8,128)} %copy-done.29), kind=kOutput, calls=%fused_computation.152 | output fusion | flops 2865167 | bytes 4492800 | tf_op jit(solution)/shard_map/sub | solution.py:83
  88.1 1.3 multiply_reduce_fusion.4
  91.1 1.2 fusion.97
  92.4 1.3 copy.196
  93.9 3.7 collective-permute-done.4
  99.8 4.8 %collective-permute-done.5 = bf16[1,8,3,12,192]{4,3,2,1,0:T(8,128)(2,1)S(1)} collective-permute-done((bf16[1,8,3,12,192]{4,3,2,1,0:T(8,128)(2,1)S(1)}, bf16[1,8,3,12,192]{4,3,2,1,0:T(8,128)(2,1)S(1)}, u32[]{:S(2)}, u32[]{:S(2)}) %collective-permute-start.5) | collective-permute-done | bytes 110624 | tf_op jit(solution)/shard_map/ppermute | solution.py:14
  106.3 3.5 fusion.21
  109.8 2.5 fusion.36
  112.3 6.2 %fusion.20 = bf16[1,4,6,144,32]{3,4,2,1,0:T(8,128)(2,1)S(1)} fusion(bf16[3,4,6,144,32]{3,4,2,1,0:T(8,128)(2,1)S(1)} %bitcast.109, f32[4,6,144,144]{2,3,1,0:T(8,128)} %fusion.36, f32[4,6,144,144]{2,3,1,0:T(8,128)} %copy-done.4, f32[4,6,144]{2,1,0:T(8,128)S(1)} %get-tuple-element.80), kind=kOutput, calls=%fused_computation.39 | convolution fusion | flops 35448336 | bytes 14835712 | tf_op jit(solution)/shard_map/nhab,nhad->nhbd/dot_general | solution.py:89
  118.5 7.0 %fusion.24 = bf16[1,4,6,144,32]{3,4,2,1,0:T(8,128)(2,1)} fusion(bf16[3,4,6,144,32]{3,4,2,1,0:T(8,128)(2,1)S(1)} %bitcast.110, f32[4,6,144,144]{2,3,1,0:T(8,128)} %fusion.36, f32[4,6,144,144]{2,3,1,0:T(8,128)} %copy-done.4, f32[4,6,144]{2,1,0:T(8,128)S(1)} %get-tuple-element.80), kind=kOutput, calls=%fused_computation.43 | convolution fusion | flops 35448336 | bytes 14835712 | tf_op jit(solution)/shard_map/nhab,nhbd->nhad/dot_general | solution.py:86
  125.5 7.1 %fusion.93 = f32[6,144,144]{1,2,0:T(8,128)} fusion(f32[4,6,144,144]{2,3,1,0:T(8,128)} %fusion.36, f32[4,6,144,144]{2,3,1,0:T(8,128)} %copy-done.4, f32[4,6,144]{2,1,0:T(8,128)S(1)} %get-tuple-element.80), kind=kOutput, calls=%fused_computation.151 | output fusion | flops 2865167 | bytes 4492800 | tf_op jit(solution)/shard_map/sub | solution.py:83
  134.7 1.2 fusion.95
  138.1 78.5 %all-reduce = (f32[192]{0:T(256)}, f32[192]{0:T(256)}) all-reduce(f32[192]{0:T(256)S(1)} %get-tuple-element.56, f32[192]{0:T(256)S(1)} %copy-done.27), channel_id=1, replica_groups=mesh['rep'=4,'lat'=8,'lon'=8] {'rep','lat','lon'}, use_global_device_ids=true, to_apply=%region_15.16 | all-reduce | flops 384 | bytes 3072 | tf_op jit(solution)/shard_map/psum | solution.py:156
  216.6 186.4 %all-reduce.4.cloned.1.call-done = (f32[192,576]{1,0:T(8,128)}, f32[192,192]{1,0:T(8,128)}, f32[6,144,144]{1,2,0:T(8,128)}, f32[192,576]{1,0:T(8,128)}, f32[192,192]{1,0:T(8,128)}, /*index=5*/f32[6,144,144]{1,2,0:T(8,128)}) async-done(((f32[192,576]{1,0:T(8,128)}, f32[192,192]{1,0:T(8,128)}, f32[6,144,144]{1,2,0:T(8,128)}, f32[192,576]{1,0:T(8,128)}, f32[192,192]{1,0:T(8,128)}, ...) | async-done | bytes 2174992 | tf_op jit(solution)/shard_map/psum | solution.py:156
  403.0 2.6 copy.198
  405.6 2.5 copy.199
  (161 shorter events, 36.2 us)
Async XLA Ops:
  7.2 43.5 %copy-start = (bf16[192,576]{1,0:T(8,128)(2,1)S(1)}, bf16[192,576]{1,0:T(8,128)(2,1)}, u32[]{:S(2)}) copy-start(bf16[192,576]{1,0:T(8,128)(2,1)} %param.17) | copy-start | bytes 663556
  7.2 10.6 %copy-start.25 = (f32[192]{0:T(256)S(1)}, f32[192]{0:T(256)}, u32[]{:S(2)}) copy-start(f32[192]{0:T(256)} %param.12) | copy-start | bytes 2308
  7.2 10.6 %copy-start.11 = (bf16[192,576]{1,0:T(8,128)(2,1)S(1)}, bf16[192,576]{1,0:T(8,128)(2,1)}, u32[]{:S(2)}) copy-start(bf16[192,576]{1,0:T(8,128)(2,1)} %param.13) | copy-start | bytes 663556
  7.2 395.7 %all-reduce.4.cloned.1.call-start = ((), (), s32[]{:S(2)}) async-start(), calls=%async_computation | async-start | bytes 6291456 | tf_op jit(solution)/shard_map/psum | solution.py:156
  9.0 32.1 %collective-permute-start = (bf16[1,8,3,12,192]{4,1,3,2,0:T(8,128)(2,1)}, bf16[1,8,3,12,192]{4,1,3,2,0:T(8,128)(2,1)}, u32[]{:S(2)}, u32[]{:S(2)}) collective-permute-start(bf16[1,8,3,12,192]{4,1,3,2,0:T(8,128)(2,1)} %get-tuple-element.79), channel_id=1, source_target_pairs={{0,56},{8,0},{16,8},{24,16},{32,24},{40,32},{48,40},{56,48},{1,57}... | collective-permute-start | bytes 331784 | tf_op jit(solution)/shard_map/ppermute | solution.py:14
  22.8 4.1 copy-start.2
  27.0 2.3 copy-start.19
  28.7 4.7 %copy-start.13 = (f32[6,144,144]{2,1,0:T(8,128)S(1)}, f32[6,144,144]{2,1,0:T(8,128)}, u32[]{:S(2)}) copy-start(f32[6,144,144]{2,1,0:T(8,128)} %param.19) | copy-start | bytes 1492996
  29.3 5.4 %copy-start.5 = (bf16[576,192]{0,1:T(8,128)(2,1)}, bf16[576,192]{0,1:T(8,128)(2,1)S(1)}, u32[]{:S(2)}) copy-start(bf16[576,192]{0,1:T(8,128)(2,1)S(1)} %reshape.362) | copy-start | bytes 663556
  29.9 5.5 %collective-permute-start.2 = (bf16[1,8,3,12,192]{4,3,2,1,0:T(8,128)(2,1)S(1)}, bf16[1,8,3,12,192]{4,3,2,1,0:T(8,128)(2,1)S(1)}, u32[]{:S(2)}, u32[]{:S(2)}) collective-permute-start(bf16[1,8,3,12,192]{4,3,2,1,0:T(8,128)(2,1)S(1)} %get-tuple-element.75), channel_id=1, source_target_pairs={{0,56},{8,0},{16,8},{24,16},{32,24},{40,32},{48,40},{56,48},{1,57}... | collective-permute-start | bytes 331784 | tf_op jit(solution)/shard_map/ppermute | solution.py:14
  35.5 8.3 %collective-permute-start.3 = (bf16[1,8,6,6,192]{4,3,2,1,0:T(8,128)(2,1)S(1)}, bf16[1,8,6,6,192]{4,3,2,1,0:T(8,128)(2,1)S(1)}, u32[]{:S(2)}, u32[]{:S(2)}) collective-permute-start(bf16[1,8,6,6,192]{4,3,2,1,0:T(8,128)(2,1)S(1)} %get-tuple-element.73), channel_id=1, source_target_pairs={{0,7},{1,0},{2,1},{3,2},{4,3},{5,4},{6,5},{7,6},{8,15},{9,8},{10,9... | collective-permute-start | bytes 331784 | tf_op jit(solution)/shard_map/ppermute | solution.py:14
  42.1 5.8 %copy-start.23 = (bf16[192,192]{1,0:T(8,128)(2,1)S(1)}, bf16[192,192]{1,0:T(8,128)(2,1)}, u32[]{:S(2)}) copy-start(bf16[192,192]{1,0:T(8,128)(2,1)} %param.18) | copy-start | bytes 221188
  42.1 4.5 %collective-permute-start.1 = (bf16[1,8,6,6,192]{4,1,3,2,0:T(8,128)(2,1)S(1)}, bf16[1,8,6,6,192]{4,1,3,2,0:T(8,128)(2,1)S(1)}, u32[]{:S(2)}, u32[]{:S(2)}) collective-permute-start(bf16[1,8,6,6,192]{4,1,3,2,0:T(8,128)(2,1)S(1)} %get-tuple-element.77), channel_id=1, source_target_pairs={{0,7},{1,0},{2,1},{3,2},{4,3},{5,4},{6,5},{7,6},{8,15},{9,8},{10,9... | collective-permute-start | bytes 331784 | tf_op jit(solution)/shard_map/ppermute | solution.py:14
  43.9 5.5 %copy-start.24 = (f32[192]{0:T(256)S(1)}, f32[192]{0:T(256)}, u32[]{:S(2)}) copy-start(f32[192]{0:T(256)} %param.16) | copy-start | bytes 2308
  53.6 4.9 %copy-start.7 = (bf16[4,144,3,6,32]{1,4,3,0,2:T(8,128)(2,1)S(1)}, bf16[4,144,3,6,32]{1,4,3,0,2:T(8,128)(2,1)}, u32[]{:S(2)}) copy-start(bf16[4,144,3,6,32]{1,4,3,0,2:T(8,128)(2,1)} %copy.232) | copy-start | bytes 1990660
  58.4 3.3 copy-start.29
  58.4 3.3 copy-start.8
  58.4 3.3 copy-start.28
  78.7 7.3 %copy-start.17 = (bf16[1,4,6,144,32]{3,4,2,1,0:T(8,128)(2,1)S(1)}, bf16[1,4,6,144,32]{3,4,2,1,0:T(8,128)(2,1)}, u32[]{:S(2)}) copy-start(bf16[1,4,6,144,32]{3,4,2,1,0:T(8,128)(2,1)} %fusion.23) | copy-start | bytes 663556
  88.1 2.7 copy-start.9
  91.0 13.7 %copy-start.6 = (bf16[576,192]{0,1:T(8,128)(2,1)S(1)}, bf16[576,192]{0,1:T(8,128)(2,1)}, u32[]{:S(2)}) copy-start(bf16[576,192]{0,1:T(8,128)(2,1)} %copy-done.5) | copy-start | bytes 663556
  91.0 14.6 %copy-start.20 = (bf16[192,192]{1,0:T(8,128)(2,1)S(1)}, bf16[192,192]{1,0:T(8,128)(2,1)}, u32[]{:S(2)}) copy-start(bf16[192,192]{1,0:T(8,128)(2,1)} %param.14) | copy-start | bytes 221188
  91.1 6.5 %collective-permute-start.4 = (bf16[1,8,6,6,192]{4,3,2,1,0:T(8,128)(2,1)S(1)}, bf16[1,8,6,6,192]{4,3,2,1,0:T(8,128)(2,1)S(1)}, u32[]{:S(2)}, u32[]{:S(2)}) collective-permute-start(bf16[1,8,6,6,192]{4,3,2,1,0:T(8,128)(2,1)S(1)} %fusion.55), channel_id=1, source_target_pairs={{0,1},{1,2},{2,3},{3,4},{4,5},{5,6},{6,7},{7,0},{8,9},{9,10},{10,1... | collective-permute-start | bytes 331784 | tf_op jit(solution)/shard_map/ppermute | solution.py:14
  97.8 6.7 %collective-permute-start.5 = (bf16[1,8,3,12,192]{4,3,2,1,0:T(8,128)(2,1)S(1)}, bf16[1,8,3,12,192]{4,3,2,1,0:T(8,128)(2,1)S(1)}, u32[]{:S(2)}, u32[]{:S(2)}) collective-permute-start(bf16[1,8,3,12,192]{4,3,2,1,0:T(8,128)(2,1)S(1)} %get-tuple-element.70), channel_id=1, source_target_pairs={{0,8},{8,16},{16,24},{24,32},{32,40},{40,48},{48,56},{56,0},{1,9},... | collective-permute-start | bytes 331784 | tf_op jit(solution)/shard_map/ppermute | solution.py:14
  106.3 3.6 copy-start.3
  125.5 7.1 %copy-start.16 = (bf16[1,4,6,144,32]{3,4,2,1,0:T(8,128)(2,1)S(1)}, bf16[1,4,6,144,32]{3,4,2,1,0:T(8,128)(2,1)}, u32[]{:S(2)}) copy-start(bf16[1,4,6,144,32]{3,4,2,1,0:T(8,128)(2,1)} %fusion.21) | copy-start | bytes 663556
  125.5 7.1 %copy-start.18 = (bf16[1,4,6,144,32]{3,4,2,1,0:T(8,128)(2,1)S(1)}, bf16[1,4,6,144,32]{3,4,2,1,0:T(8,128)(2,1)}, u32[]{:S(2)}) copy-start(bf16[1,4,6,144,32]{3,4,2,1,0:T(8,128)(2,1)} %fusion.24) | copy-start | bytes 663556
  133.9 2.3 copy-start.12
  403.0 5.2 %copy-start.15 = (f32[192,576]{1,0:T(8,128)S(1)}, f32[192,576]{1,0:T(8,128)}, u32[]{:S(2)}) copy-start(f32[192,576]{1,0:T(8,128)} %get-tuple-element.90) | copy-start | bytes 1327108
  403.0 5.9 %copy-start.22 = (f32[192,192]{1,0:T(8,128)S(1)}, f32[192,192]{1,0:T(8,128)}, u32[]{:S(2)}) copy-start(f32[192,192]{1,0:T(8,128)} %get-tuple-element.91) | copy-start | bytes 442372
  403.0 6.6 %copy-start.14 = (f32[192,576]{1,0:T(8,128)S(1)}, f32[192,576]{1,0:T(8,128)}, u32[]{:S(2)}) copy-start(f32[192,576]{1,0:T(8,128)} %get-tuple-element.94) | copy-start | bytes 1327108
  403.0 7.4 %copy-start.21 = (f32[192,192]{1,0:T(8,128)S(1)}, f32[192,192]{1,0:T(8,128)}, u32[]{:S(2)}) copy-start(f32[192,192]{1,0:T(8,128)} %get-tuple-element.95) | copy-start | bytes 442372
  (5 other events, 10.2 us)
Sparse Core Ops, SparseCore 0:
  136.1 266.8 all-reduce.3
where the time goes:
time: 426 us; the launch traced here: 418 us
  waiting for transfers between devices  198 us (46%)
  blocking collectives  78.5 us (18%)
  matrix products  53.3 us (13%)
  local copies, waits for them, and re-layouts  35.2 us (8%)
  other arithmetic  25.2 us (6%)
  between operations  15.2 us (4%)
  starting transfers between devices  12.8 us (3%)
    psum x1, waiting for transfers between devices, local(): lax.psum((grads_a[0], grads_a[1], grads_a[2], grads_a[3], grads_b[0], gra...  186 us
    psum x1, blocking collectives, local(): lax.psum((grads_a[0], grads_a[1], grads_a[2], grads_a[3], grads_b[0], gra...  78.5 us
    sub x2, other arithmetic, attend_backward(): d_probs - jnp.sum(probs * d_probs, axis=-1, keepdims=True)  14.4 us
    dot_general x2, matrix products, attend_backward(): jnp.einsum('nhab,nhbd->nhad', d_scaled, key, preferred_element_type=jnp.f...  14.3 us
    unnamed x69, local copies, waits for them, and re-layouts  13.8 us
    ppermute x6, starting transfers between devices, from_behind(): return lax.ppermute(value, axis, pairs)  12.7 us
    dot_general x2, matrix products, attend_backward(): jnp.einsum('nhab,nhad->nhbd', d_scaled, query, preferred_element_type=jnp...  12.6 us
    ppermute x6, waiting for transfers between devices, from_behind(): return lax.ppermute(value, axis, pairs)  11.7 us
  transfers between devices with their start and end apart: 7, of which 6 were waited for; matrix products, arithmetic and copies ran while one was open for 6% of the time, Pallas kernels for 0%

commit v1 on v0

v1 whole, which is shorter than its diff:
```python
import functools

import jax
import jax.numpy as jnp
import numpy as np
from jax import lax
from jax.experimental import pallas as pl
from jax.experimental.pallas import tpu as pltpu
from jax.sharding import PartitionSpec as P

MESH = pl.DeviceIdType.MESH
C = 192
HEADS = 6
HEAD = 32
WT = 144
LEVELS = 8
WINDOWS = 4
TOK = WT * WINDOWS
FACTOR = HEAD ** (-0.5)
F32 = jnp.float32
BF16 = jnp.bfloat16
PIECE = 144
SPOTS = 16
HALF = PIECE * SPOTS
VMEM_LIMIT = 48 * 1024 * 1024


def nt(left, right):
    return lax.dot_general(left, right, (((1,), (1,)), ((), ())), preferred_element_type=F32)


def tn(left, right):
    return lax.dot_general(left, right, (((0,), (0,)), ((), ())), preferred_element_type=F32)


def nn(left, right):
    return lax.dot_general(left, right, (((1,), (0,)), ((), ())), preferred_element_type=F32)


def routes():
    slot_of_token = np.zeros(TOK, np.int32)
    place_of_slot = np.zeros(TOK, np.int32)
    for z in range(8):
        for i in range(6):
            for j in range(12):
                token = z * 72 + i * 12 + j
                zr, ir, jr = (z - 1) % 8, (i + 3) % 6, (j + 6) % 12
                quarter = 2 * (ir >= 3) + (jr >= 6)
                slot = quarter * WT + zr * 18 + (ir % 3) * 6 + jr % 6
                slot_of_token[token] = slot
                place_of_slot[slot] = zr * 72 + ir * 12 + jr
    return np.stack(
        [slot_of_token, place_of_slot, np.argsort(place_of_slot), np.argsort(slot_of_token)]
    ).astype(np.int32)


def head_mask(h, dtype):
    lane = lax.broadcasted_iota(jnp.int32, (1, C), 1)
    return jnp.where((lane >= h * HEAD) & (lane < (h + 1) * HEAD), 1.0, 0.0).astype(dtype)


def window_forward(w, x, gain, wq, wk, wv, bias, extra, save):
    unit_s, inv_s, normed_s, q_s, k_s, v_s, p_s, att_s = save
    rows = pl.ds(pl.multiple_of(w * WT, WT), WT)
    xf = x.astype(F32)
    center = xf - jnp.mean(xf, axis=-1, keepdims=True)
    inv = lax.rsqrt(jnp.mean(center * center, axis=-1, keepdims=True) + 1e-05)
    unit = center * inv
    normed = (unit * gain).astype(BF16)
    unit_s[rows, :] = unit
    inv_s[rows, :] = inv
    normed_s[rows, :] = normed
    q = nn(normed, wq).astype(BF16)
    k = nn(normed, wk).astype(BF16)
    v = nn(normed, wv).astype(BF16)
    q_s[rows, :] = q
    k_s[rows, :] = k
    v_s[rows, :] = v
    att = jnp.zeros((WT, C), F32)
    for h in range(HEADS):
        m = head_mask(h, BF16)
        s = nt(q * m, k) * FACTOR + bias[h]
        if extra is not None:
            s = s + extra
        e = jnp.exp(s - jnp.max(s, axis=-1, keepdims=True))
        p = (e * (1.0 / jnp.sum(e, axis=-1, keepdims=True))).astype(BF16)
        p_s[w * HEADS + h] = p
        att = att + nn(p, v * m)
    att = att.astype(BF16)
    att_s[rows, :] = att
    return xf, att


def window_backward(w, g, gain, wq, wk, wv, wo, save, grads):
    unit_s, inv_s, normed_s, q_s, k_s, v_s, p_s, att_s = save
    gq_s, gk_s, gv_s, go_s, gb_s, gg_s = grads
    rows = pl.ds(pl.multiple_of(w * WT, WT), WT)
    go_s[...] += tn(att_s[rows, :], g)
    da = nt(g, wo).astype(BF16)
    q = q_s[rows, :]
    k = k_s[rows, :]
    v = v_s[rows, :]
    dq = jnp.zeros((WT, C), F32)
    dk = jnp.zeros((WT, C), F32)
    dv = jnp.zeros((WT, C), F32)
    for h in range(HEADS):
        m = head_mask(h, BF16)
        dah = da * m
        p = p_s[w * HEADS + h]
        dp = nt(dah, v)
        pf = p.astype(F32)
        t = pf * dp
        ds = t - pf * jnp.sum(t, axis=-1, keepdims=True)
        gb_s[h] += ds
        dsb = (ds * FACTOR).astype(BF16)
        dv = dv + tn(p, dah)
        dq = dq + nn(dsb, k * m)
        dk = dk + tn(dsb, q * m)
    dq = dq.astype(BF16)
    dk = dk.astype(BF16)
    dv = dv.astype(BF16)
    normed = normed_s[rows, :]
    gq_s[...] += tn(normed, dq)
    gk_s[...] += tn(normed, dk)
    gv_s[...] += tn(normed, dv)
    dn = nt(dq, wq) + nt(dk, wk) + nt(dv, wv)
    unit = unit_s[rows, :]
    gg_s[...] += jnp.sum(dn * unit, axis=0, keepdims=True)
    dh = dn * gain
    d_in = g.astype(F32) + inv_s[rows, :] * (
        dh
        - jnp.mean(dh, axis=-1, keepdims=True)
        - unit * jnp.mean(dh * unit, axis=-1, keepdims=True)
    )
    return d_in.astype(BF16)


def pack(out, base, grads):
    gq_s, gk_s, gv_s, go_s, gb_s, gg_s = grads
    at = base
    for ref in (gq_s, gk_s, gv_s, go_s):
        out[at : at + C, :] = ref[:, :128].astype(BF16)
        at += C
    for one, two in ((gq_s, gk_s), (gv_s, go_s)):
        out[at : at + C, :] = jnp.concatenate([one[:, 128:], two[:, 128:]], axis=1).astype(BF16)
        at += C
    for h in range(HEADS):
        out[at : at + WT, :] = gb_s[h, :, :128].astype(BF16)
        at += WT
    tails = [gb_s[h, :, 128:] for h in range(HEADS)] + [jnp.zeros((WT, 32), F32)]
    out[at : at + WT, :] = jnp.concatenate(tails, axis=1).astype(BF16)
    at += WT
    gg = gg_s[...]
    second = jnp.concatenate([gg[:, 128:], jnp.zeros((1, 64), F32)], axis=1)
    tile = jnp.concatenate([gg[:, :128], second, jnp.zeros((14, 128), F32)], axis=0)
    out[at : at + 16, :] = tile.astype(BF16)
    at += 16
    out[at : base + HALF, :] = jnp.zeros((base + HALF - at, 128), BF16)


def layer_kernel(
    lats,
    lons,
    tok_ref,
    cot_ref,
    gain_a,
    qkv_a,
    out_a,
    bias_a,
    gain_b,
    qkv_b,
    out_b,
    bias_b,
    route_ref,
    dtok_ref,
    grads_ref,
    save_a,
    save_b,
    grad_a,
    grad_b,
    mat_s,
    extra_s,
    mid_s,
    send_s,
    recv_s,
    x_b,
    g_b,
    send_sem,
    recv_sem,
):
    lat = lax.axis_index("lat")
    lon = lax.axis_index("lon")

    def shifted(dlat, dlon):
        return {"lat": lax.rem(lat + dlat + lats, lats), "lon": lax.rem(lon + dlon + lons, lons)}

    before = [shifted(0, -1), shifted(-1, 0), shifted(-1, -1)]
    after = [shifted(0, 1), shifted(1, 0), shifted(1, 1)]

    def quarters(leg, targets):
        copies = []
        for n, target in enumerate(targets):
            rows = pl.ds((n + 1) * WT, WT)
            copies.append(
                pltpu.make_async_remote_copy(
                    src_ref=send_s.at[leg, rows],
                    dst_ref=recv_s.at[leg, rows],
                    send_sem=send_sem.at[leg * 3 + n],
                    recv_sem=recv_sem.at[leg * 3 + n],
                    device_id=target,
                    device_id_type=MESH,
                )
            )
        return copies

    barrier = pltpu.get_barrier_semaphore()
    for other in before + after:
        pl.semaphore_signal(barrier, inc=1, device_id=other, device_id_type=MESH)

    row_iota = lax.broadcasted_iota(jnp.int32, (TOK, TOK), 0)
    for n in range(4):
        mat_s[n] = jnp.where(row_iota == route_ref[n : n + 1, :], 1.0, 0.0).astype(BF16)

    send_s[0] = nn(mat_s[0], cot_ref[...]).astype(BF16)
    pl.semaphore_wait(barrier, 6)
    legs = [quarters(0, before), quarters(1, before), quarters(2, after)]
    for copy in legs[0]:
        copy.start()
    recv_s[0, 0:WT] = send_s[0, 0:WT]

    for grads in (grad_a, grad_b):
        for ref in grads:
            ref[...] = jnp.zeros_like(ref)

    def label(shape, axis, level):
        at = lax.broadcasted_iota(jnp.int32, shape, axis)
        upper = jnp.where(at >= 72, 1, 0)
        inside = at - 72 * upper
        late = jnp.where(inside >= 36, 1, 0) * jnp.where(lat == lats - 1, 1, 0)
        return late + 2 * upper if level else late

    for n in range(2):
        same = label((WT, WT), 0, n) == label((WT, WT), 1, n)
        extra_s[n] = jnp.where(same, 0.0, -1e30)

    ga = gain_a[...]
    wo = out_a[...]
    wqa, wka, wva = (qkv_a[:, n * C : (n + 1) * C] for n in range(3))

    def regular(w, carry):
        rows = pl.ds(pl.multiple_of(w * WT, WT), WT)
        xf, att = window_forward(w, tok_ref[rows, :], ga, wqa, wka, wva, bias_a, None, save_a)
        mid_s[rows, :] = (xf + nn(att, wo)).astype(BF16)
        return carry

    lax.fori_loop(0, WINDOWS, regular, 0)

    send_s[1] = nn(mat_s[0], mid_s[...]).astype(BF16)
    for copy in legs[1]:
        copy.start()
    recv_s[1, 0:WT] = send_s[1, 0:WT]
    for copy in legs[0]:
        copy.wait()
    g_b[...] = nn(mat_s[1], recv_s[0]).astype(BF16)
    for copy in legs[1]:
        copy.wait()
    x_b[...] = nn(mat_s[1], recv_s[1]).astype(BF16)

    gb = gain_b[...]
    wob = out_b[...]
    wqb, wkb, wvb = (qkv_b[:, n * C : (n + 1) * C] for n in range(3))

    def shifted_block(w, carry):
        rows = pl.ds(pl.multiple_of(w * WT, WT), WT)
        extra = extra_s[lax.div(w, WINDOWS - 1)]
        window_forward(w, x_b[rows, :], gb, wqb, wkb, wvb, bias_b, extra, save_b)
        x_b[rows, :] = window_backward(w, g_b[rows, :], gb, wqb, wkb, wvb, wob, save_b, grad_b)
        return carry

    lax.fori_loop(0, WINDOWS, shifted_block, 0)

    send_s[2] = nn(mat_s[2], x_b[...]).astype(BF16)
    for copy in legs[2]:
        copy.start()
    recv_s[2, 0:WT] = send_s[2, 0:WT]
    pack(grads_ref, HALF, grad_b)
    for copy in legs[2]:
        copy.wait()
    mid_s[...] = nn(mat_s[3], recv_s[2]).astype(BF16)

    def regular_back(w, carry):
        rows = pl.ds(pl.multiple_of(w * WT, WT), WT)
        dtok_ref[rows, :] = window_backward(w, mid_s[rows, :], ga, wqa, wka, wva, wo, save_a, grad_a)
        return carry

    lax.fori_loop(0, WINDOWS, regular_back, 0)
    pack(grads_ref, 0, grad_a)


def sum_kernel(
    in_ref,
    out_ref,
    core_s,
    part_s,
    plane_s,
    line_s,
    core_send,
    core_recv,
    plane_send,
    plane_recv,
    line_send,
    line_recv,
    back_send,
    back_recv,
    last_send,
    last_recv,
):
    rep = lax.axis_index("rep")
    lat = lax.axis_index("lat")
    lon = lax.axis_index("lon")
    x_hi, core = rep // 2, rep % 2
    x_lo, y = lat // 4, lat % 4
    me = (x_hi * 2 + x_lo) * 4 + y
    partner = {"rep": x_hi * 2 + (1 - core)}

    def spot(index):
        x, yy = index // 4, index % 4
        return {"rep": (x // 2) * 2 + core, "lat": (x % 2) * 4 + yy}

    barrier = pltpu.get_barrier_semaphore()
    pl.semaphore_signal(barrier, inc=1, device_id=partner, device_id_type=MESH)

    def greet_plane(k, carry):
        pl.semaphore_signal(
            barrier, inc=1, device_id=spot(lax.rem(me + k, SPOTS)), device_id_type=MESH
        )
        return carry

    def greet_line(k, carry):
        pl.semaphore_signal(
            barrier, inc=1, device_id={"lon": lax.rem(lon + k, 8)}, device_id_type=MESH
        )
        return carry

    lax.fori_loop(1, SPOTS, greet_plane, 0)
    lax.fori_loop(1, 8, greet_line, 0)
    pl.semaphore_wait(barrier, 1 + SPOTS - 1 + 7)

    def core_copy(k):
        j = lax.rem(me + k, SPOTS)
        return pltpu.make_async_remote_copy(
            src_ref=in_ref.at[1 - core, j],
            dst_ref=core_s.at[k],
            send_sem=core_send.at[k],
            recv_sem=core_recv.at[k],
            device_id=partner,
            device_id_type=MESH,
        )

    def plane_copy(k):
        return pltpu.make_async_remote_copy(
            src_ref=part_s.at[k],
            dst_ref=plane_s.at[k],
            send_sem=plane_send.at[k],
            recv_sem=plane_recv.at[k],
            device_id=spot(lax.rem(me + k, SPOTS)),
            device_id_type=MESH,
        )

    def start_core(k, carry):
        core_copy(k).start()
        return carry

    lax.fori_loop(1, SPOTS, start_core, 0)
    core_copy(0).start()

    def merge_core(k):
        core_copy(k).wait()
        j = lax.rem(me + k, SPOTS)
        return in_ref[core, j].astype(F32) + core_s[k].astype(F32)

    def start_plane(k, carry):
        part_s[k] = merge_core(k).astype(BF16)
        plane_copy(k).start()
        return carry

    lax.fori_loop(1, SPOTS, start_plane, 0)

    def add_plane(k, total):
        plane_copy(k).wait()
        return total + plane_s[k].astype(F32)

    total = lax.fori_loop(1, SPOTS, add_plane, merge_core(0))
    line_s[lon] = total.astype(BF16)

    def line_copy(k):
        return pltpu.make_async_remote_copy(
            src_ref=line_s.at[lon],
            dst_ref=line_s.at[lon],
            send_sem=line_send.at[k],
            recv_sem=line_recv.at[k],
            device_id={"lon": lax.rem(lon + k, 8)},
            device_id_type=MESH,
        )

    def start_line(k, carry):
        line_copy(k).start()
        return carry

    def wait_line(k, carry):
        line_copy(k).wait_send()
        pltpu.make_async_remote_copy(
            src_ref=line_s.at[lax.rem(lon + 8 - k, 8)],
            dst_ref=line_s.at[lax.rem(lon + 8 - k, 8)],
            send_sem=line_send.at[k],
            recv_sem=line_recv.at[k],
            device_id={"lon": lax.rem(lon + k, 8)},
            device_id_type=MESH,
        ).wait_recv()
        return carry

    lax.fori_loop(1, 8, start_line, 0)
    lax.fori_loop(1, 8, wait_line, 0)
    total = line_s[0].astype(F32)
    for n in range(1, 8):
        total = total + line_s[n].astype(F32)
    out_ref[core, me] = total.astype(BF16)

    def back_copy(k, j):
        return pltpu.make_async_remote_copy(
            src_ref=out_ref.at[core, j],
            dst_ref=out_ref.at[core, j],
            send_sem=back_send.at[k],
            recv_sem=back_recv.at[k],
            device_id=spot(lax.rem(me + k, SPOTS)),
            device_id_type=MESH,
        )

    def last_copy(k, half):
        j = lax.rem(me + SPOTS - k, SPOTS)
        return pltpu.make_async_remote_copy(
            src_ref=out_ref.at[half, j],
            dst_ref=out_ref.at[half, j],
            send_sem=last_send.at[k],
            recv_sem=last_recv.at[k],
            device_id=partner,
            device_id_type=MESH,
        )

    def start_back(k, carry):
        back_copy(k, me).start()
        return carry

    def forward(k, carry):
        back_copy(k, me).wait_send()
        back_copy(k, lax.rem(me + SPOTS - k, SPOTS)).wait_recv()
        last_copy(k, core).start()
        return carry

    def finish(k, carry):
        last_copy(k, core).wait_send()
        last_copy(k, 1 - core).wait_recv()
        return carry

    lax.fori_loop(1, SPOTS, start_back, 0)
    last_copy(0, core).start()
    lax.fori_loop(1, SPOTS, forward, 0)
    lax.fori_loop(0, SPOTS, finish, 0)


def unpack_kernel(in_ref, *outs):
    for block in range(2):
        gain, qkv, out, bias = outs[4 * block : 4 * block + 4]
        at = block * HALF

        def rows(count):
            nonlocal at
            at += count
            return in_ref[at - count : at, :].astype(F32)

        gq, gk, gv, go = (rows(C) for _ in range(4))
        one, two = rows(C), rows(C)
        qkv[...] = jnp.concatenate(
            [gq, one[:, :64], gk, one[:, 64:], gv, two[:, :64]], axis=1
        )
        out[...] = jnp.concatenate([go, two[:, 64:]], axis=1)
        main = [rows(WT) for _ in range(HEADS)]
        tails = rows(WT)
        for h in range(HEADS):
            bias[h] = jnp.concatenate([main[h], tails[:, 16 * h : 16 * h + 16]], axis=1)
        last = rows(16)
        gain[...] = jnp.concatenate([last[0:1, :], last[1:2, :64]], axis=1)


def saves():
    return (
        pltpu.VMEM((TOK, C), F32),
        pltpu.VMEM((TOK, 1), F32),
        pltpu.VMEM((TOK, C), BF16),
        pltpu.VMEM((TOK, C), BF16),
        pltpu.VMEM((TOK, C), BF16),
        pltpu.VMEM((TOK, C), BF16),
        pltpu.VMEM((WINDOWS * HEADS, WT, WT), BF16),
        pltpu.VMEM((TOK, C), BF16),
    )


def totals():
    return (
        pltpu.VMEM((C, C), F32),
        pltpu.VMEM((C, C), F32),
        pltpu.VMEM((C, C), F32),
        pltpu.VMEM((C, C), F32),
        pltpu.VMEM((HEADS, WT, WT), F32),
        pltpu.VMEM((1, C), F32),
    )


def run_layer(lats, lons, *args):
    return pl.pallas_call(
        functools.partial(layer_kernel, lats, lons),
        out_shape=(
            jax.ShapeDtypeStruct((TOK, C), BF16),
            jax.ShapeDtypeStruct((2 * HALF, 128), BF16),
        ),
        in_specs=[pl.BlockSpec(memory_space=pltpu.VMEM)] * 11,
        out_specs=(pl.BlockSpec(memory_space=pltpu.VMEM),) * 2,
        scratch_shapes=[
            saves(),
            saves(),
            totals(),
            totals(),
            pltpu.VMEM((4, TOK, TOK), BF16),
            pltpu.VMEM((2, WT, WT), F32),
            pltpu.VMEM((TOK, C), BF16),
            pltpu.VMEM((3, TOK, C), BF16),
            pltpu.VMEM((3, TOK, C), BF16),
            pltpu.VMEM((TOK, C), BF16),
            pltpu.VMEM((TOK, C), BF16),
            pltpu.SemaphoreType.DMA((9,)),
            pltpu.SemaphoreType.DMA((9,)),
        ],
        compiler_params=pltpu.CompilerParams(
            collective_id=0, has_side_effects=True, vmem_limit_bytes=VMEM_LIMIT
        ),
        name="layer",
    )(*args)


def run_sum(value):
    piece = (PIECE, 128)
    return pl.pallas_call(
        sum_kernel,
        out_shape=jax.ShapeDtypeStruct((2, SPOTS) + piece, BF16),
        in_specs=[pl.BlockSpec(memory_space=pltpu.VMEM)],
        out_specs=pl.BlockSpec(memory_space=pltpu.VMEM),
        scratch_shapes=[
            pltpu.VMEM((SPOTS,) + piece, BF16),
            pltpu.VMEM((SPOTS,) + piece, BF16),
            pltpu.VMEM((SPOTS,) + piece, BF16),
            pltpu.VMEM((8,) + piece, BF16),
        ]
        + [pltpu.SemaphoreType.DMA((SPOTS,))] * 4
        + [pltpu.SemaphoreType.DMA((8,))] * 2
        + [pltpu.SemaphoreType.DMA((SPOTS,))] * 4,
        compiler_params=pltpu.CompilerParams(
            collective_id=1, has_side_effects=True, vmem_limit_bytes=VMEM_LIMIT
        ),
        name="gradient_sum",
    )(value)


def run_unpack(value):
    block = (
        jax.ShapeDtypeStruct((1, C), F32),
        jax.ShapeDtypeStruct((C, 3 * C), F32),
        jax.ShapeDtypeStruct((C, C), F32),
        jax.ShapeDtypeStruct((HEADS, WT, WT), F32),
    )
    return pl.pallas_call(
        unpack_kernel,
        out_shape=block + block,
        in_specs=[pl.BlockSpec(memory_space=pltpu.VMEM)],
        out_specs=(pl.BlockSpec(memory_space=pltpu.VMEM),) * 8,
        compiler_params=pltpu.CompilerParams(vmem_limit_bytes=VMEM_LIMIT),
        name="unpack",
    )(value)


def solution(mesh):
    lats, lons = mesh.shape["lat"], mesh.shape["lon"]
    route = routes()

    def local(tokens, cotangent, gain_a, qkv_a, out_a, bias_a, gain_b, qkv_b, out_b, bias_b):
        d_tokens, packed = run_layer(
            lats,
            lons,
            tokens.reshape(TOK, C),
            cotangent.reshape(TOK, C),
            gain_a.reshape(1, C),
            qkv_a,
            out_a,
            bias_a,
            gain_b.reshape(1, C),
            qkv_b,
            out_b,
            bias_b,
            jnp.asarray(route),
        )
        summed = run_sum(packed.reshape(2, SPOTS, PIECE, 128))
        res = run_unpack(summed.reshape(2 * HALF, 128))
        ga, qa, oa, ba, gb, qb, ob, bb = res
        return (
            d_tokens.reshape(tokens.shape),
            ga.reshape(C),
            qa,
            oa,
            ba,
            gb.reshape(C),
            qb,
            ob,
            bb,
        )

    grid = P("rep", None, "lat", "lon", None)
    return jax.shard_map(
        local,
        mesh=mesh,
        in_specs=(grid, grid) + (P(),) * 8,
        out_specs=(grid,) + (P(),) * 8,
        check_vma=False,
    )
```

time: 426 us -> 100 us (0.23); the launches traced: 418 us -> 99.9 us
  waiting for transfers between devices: 198 us -> 0 us
  Pallas kernels: 0 us -> 93.9 us
  blocking collectives: 78.5 us -> 0 us
  matrix products: 53.3 us -> 0 us
  local copies, waits for them, and re-layouts: 35.2 us -> 5.25 us
  other arithmetic: 25.2 us -> 0 us
  between operations: 15.2 us -> 0.83 us
  starting transfers between devices: 12.8 us -> 0 us
    psum x1 -> x0, waiting for transfers between devices: 186 us -> none  [local(): lax.psum((grads_a[0], grads_a[1], grads_a[2], grads_a[3], grads_b[0], gra...]
    pallas_call x0 -> x3, Pallas kernels: none -> 93.9 us  [the longest x1 53.3 us: run_layer(): pl.pallas_call(functools.partial(layer_kernel, lats, lons), out_shape=(ja...]
    psum x1 -> x0, blocking collectives: 78.5 us -> none  [local(): lax.psum((grads_a[0], grads_a[1], grads_a[2], grads_a[3], grads_b[0], gra...]
    dot_general x22 -> x0, matrix products: 48.5 us -> none  [the longest x2 14.3 us: attend_backward(): jnp.einsum('nhab,nhbd->nhad', d_scaled, key, preferred_element_type=jnp.f...]
    sub x3 -> x0, other arithmetic: 15.8 us -> none  [the longest x2 14.4 us: attend_backward(): d_probs - jnp.sum(probs * d_probs, axis=-1, keepdims=True)]
    ppermute x6 -> x0, starting transfers between devices: 12.7 us -> none  [from_behind(): return lax.ppermute(value, axis, pairs)]
    ppermute x6 -> x0, waiting for transfers between devices: 11.7 us -> none  [from_behind(): return lax.ppermute(value, axis, pairs)]
    unnamed x69 -> x21, local copies, waits for them, and re-layouts: 13.8 us -> 3.9 us
  transfers between devices with their start and end apart: 7 -> 0, of which waited for: 6 -> 0; matrix products, arithmetic and copies ran while one was open for 6% -> 0% of each run, Pallas kernels for 0% -> 0%
where the time goes in v1:
time: 100 us; the launch traced here: 99.9 us
  Pallas kernels  93.9 us (94%)
  local copies, waits for them, and re-layouts  5.25 us (5%)
    pallas_call x1, Pallas kernels, run_layer(): pl.pallas_call(functools.partial(layer_kernel, lats, lons), out_shape=(ja...  53.3 us
    pallas_call x1, Pallas kernels, run_sum(): pl.pallas_call(sum_kernel, out_shape=jax.ShapeDtypeStruct((2, SPOTS) + pi...  38.7 us
    unnamed x21, local copies, waits for them, and re-layouts  3.9 us

profile of v1, /device:TPU:1, one launch (start us, length us, event | category | flops | bytes accessed | tf_op | source)
XLA Modules:
  0.0 99.9 jit_solution(11749820614078986849)
XLA Ops:
  0.6 0.0 copy-start.3
  0.7 0.0 copy-start.4
  0.7 0.0 copy-start.5
  0.7 1.1 %copy.23 = bf16[1,8,6,12,192]{4,3,2,1,0:T(8,128)(2,1)S(1)} copy(bf16[1,8,6,12,192]{4,1,3,2,0:T(8,128)(2,1)} %param.11) | data formatting | bytes 442368 | tf_op args[0]
  1.8 0.0 copy-start
  1.8 0.0 copy-start.1
  1.8 0.0 copy-start.2
  1.8 0.0 copy-start.6
  1.8 0.0 copy-start.7
  1.8 0.0 copy-start.8
  1.8 0.1 reshape.45.tok_ref
  2.0 1.9 %copy.24 = bf16[1,8,6,12,192]{4,3,2,1,0:T(8,128)(2,1)} copy(bf16[1,8,6,12,192]{4,1,3,2,0:T(8,128)(2,1)} %param.12) | data formatting | bytes 442368 | tf_op args[1]
  3.9 1.1 %reshape.46.cot_ref = bf16[576,192]{1,0:T(8,128)(2,1)S(1)} reshape(bf16[1,8,6,12,192]{4,3,2,1,0:T(8,128)(2,1)} %copy.24) | data formatting | bytes 442368 | tf_op jit(solution)/shard_map/reshape | solution.py:599
  5.0 0.0 copy-done.3
  5.0 0.0 copy-done.4
  5.0 0.0 copy-done.5
  5.0 0.0 copy-done
  5.0 0.0 copy-done.1
  5.0 0.0 copy-done.2
  5.1 0.0 copy-done.6
  5.1 0.0 copy-done.7
  5.1 0.0 copy-done.8
  5.1 53.3 %layer.1 = (bf16[576,192]{1,0:T(8,128)(2,1)S(1)}, bf16[4608,128]{1,0:T(8,128)(2,1)S(1)}) custom-call(bf16[576,192]{1,0:T(8,128)(2,1)S(1)} %reshape.45.tok_ref, bf16[576,192]{1,0:T(8,128)(2,1)S(1)} %reshape.46.cot_ref, f32[1,192]{1,0:T(1,128)S(1)} %bitcast.8, bf16[192,576]{1,0:T(8,128)(2,1)S(1)} %copy-done.2, bf16[192,192]{1,0:T(8,128)(2,1)S(1)} %copy-done.4, ...), custom_call_target="tpu_custom_call" | custom-call | tf_op jit(solution)/shard_map/layer/pallas_call | solution.py:520
  58.4 38.7 %gradient_sum.1 = bf16[2,16,144,128]{3,2,1,0:T(8,128)(2,1)S(1)} custom-call(bf16[2,16,144,128]{3,2,1,0:T(8,128)(2,1)S(1)} %bitcast.7), custom_call_target="tpu_custom_call" | custom-call | tf_op jit(solution)/shard_map/gradient_sum/pallas_call | solution.py:552
  97.1 0.1 reshape.49
  97.2 0.9 copy.25
  98.1 1.8 %unpack.1 = (f32[1,192]{1,0:T(1,128)}, f32[192,576]{1,0:T(8,128)}, f32[192,192]{1,0:T(8,128)}, f32[6,144,144]{2,1,0:T(8,128)}, f32[1,192]{1,0:T(1,128)}, /*index...) custom-call(bf16[4608,128]{1,0:T(8,128)(2,1)S(1)} %bitcast.6), custom_call_target="tpu_custom_call" | custom-call | tf_op jit(solution)/shard_map/unpack/pallas_call | solution.py:580
Async XLA Ops:
  0.6 4.4 %copy-start.3 = (bf16[192,576]{1,0:T(8,128)(2,1)S(1)}, bf16[192,576]{1,0:T(8,128)(2,1)}, u32[]{:S(2)}) copy-start(bf16[192,576]{1,0:T(8,128)(2,1)} %qkv_b.1) | copy-start | bytes 663556
  0.7 4.4 %copy-start.4 = (bf16[192,192]{1,0:T(8,128)(2,1)S(1)}, bf16[192,192]{1,0:T(8,128)(2,1)}, u32[]{:S(2)}) copy-start(bf16[192,192]{1,0:T(8,128)(2,1)} %out_a.1) | copy-start | bytes 221188
  0.7 4.4 %copy-start.5 = (bf16[192,192]{1,0:T(8,128)(2,1)S(1)}, bf16[192,192]{1,0:T(8,128)(2,1)}, u32[]{:S(2)}) copy-start(bf16[192,192]{1,0:T(8,128)(2,1)} %out_b.1) | copy-start | bytes 221188
  1.8 3.3 %copy-start = (f32[6,144,144]{2,1,0:T(8,128)S(1)}, f32[6,144,144]{2,1,0:T(8,128)}, u32[]{:S(2)}) copy-start(f32[6,144,144]{2,1,0:T(8,128)} %bias_a.1) | copy-start | bytes 1492996
  1.8 3.3 %copy-start.1 = (f32[6,144,144]{2,1,0:T(8,128)S(1)}, f32[6,144,144]{2,1,0:T(8,128)}, u32[]{:S(2)}) copy-start(f32[6,144,144]{2,1,0:T(8,128)} %bias_b.1) | copy-start | bytes 1492996
  1.8 3.3 %copy-start.2 = (bf16[192,576]{1,0:T(8,128)(2,1)S(1)}, bf16[192,576]{1,0:T(8,128)(2,1)}, u32[]{:S(2)}) copy-start(bf16[192,576]{1,0:T(8,128)(2,1)} %qkv_a.1) | copy-start | bytes 663556
  1.8 3.3 %copy-start.6 = (s32[4,576]{1,0:T(4,128)S(1)}, s32[4,576]{1,0:T(4,128)}, u32[]{:S(2)}) copy-start(s32[4,576]{1,0:T(4,128)} %constant.2.clone.route_ref) | copy-start | bytes 27652
  1.8 3.3 %copy-start.7 = (f32[192]{0:T(256)S(1)}, f32[192]{0:T(256)}, u32[]{:S(2)}) copy-start(f32[192]{0:T(256)} %param.13) | copy-start | bytes 2308
  1.8 3.3 %copy-start.8 = (f32[192]{0:T(256)S(1)}, f32[192]{0:T(256)}, u32[]{:S(2)}) copy-start(f32[192]{0:T(256)} %param.17) | copy-start | bytes 2308

commit v2 on v1

v2 whole, which is shorter than its diff:
```python
import functools

import jax
import jax.numpy as jnp
import numpy as np
from jax import lax
from jax.experimental import pallas as pl
from jax.experimental.pallas import tpu as pltpu
from jax.sharding import PartitionSpec as P

MESH = pl.DeviceIdType.MESH
C = 192
HEADS = 6
HEAD = 32
WT = 144
LEVELS = 8
WINDOWS = 4
TOK = WT * WINDOWS
FACTOR = HEAD ** (-0.5)
F32 = jnp.float32
BF16 = jnp.bfloat16
PIECE = 80
SPOTS = 16
HALF = PIECE * SPOTS
STEP = 144
SLOT = 48
VMEM_LIMIT = 56 * 1024 * 1024


def nt(left, right):
    return lax.dot_general(left, right, (((1,), (1,)), ((), ())), preferred_element_type=F32)


def tn(left, right):
    return lax.dot_general(left, right, (((0,), (0,)), ((), ())), preferred_element_type=F32)


def nn(left, right):
    return lax.dot_general(left, right, (((1,), (0,)), ((), ())), preferred_element_type=F32)


def routes():
    out = np.full((16, TOK), -1, np.int32)
    for z in range(LEVELS):
        for i in range(6):
            for j in range(12):
                stored = (i * 12 + j) * LEVELS + z
                token = z * 72 + i * 12 + j
                out[0, stored] = token
                out[1, token] = stored
                zr, ir, jr = (z - 1) % LEVELS, (i + 3) % 6, (j + 6) % 12
                quarter = 2 * (ir >= 3) + (jr >= 6)
                window, level = zr // 2, zr % 2
                inside = level * 18 + (ir % 3) * 6 + jr % 6
                slot = quarter * SLOT + inside
                place = level * 72 + ir * 12 + jr
                column = i * 12 + j
                out[2, stored] = (quarter * WINDOWS + window) * SLOT + inside
                out[3 + level, column] = slot
                out[5, slot] = place
                out[6, place] = slot
                out[7 + level, slot] = column
    return out


def head_mask(h, dtype):
    lane = lax.broadcasted_iota(jnp.int32, (1, C), 1)
    return jnp.where((lane >= h * HEAD) & (lane < (h + 1) * HEAD), 1.0, 0.0).astype(dtype)


def spread(value):
    return jnp.concatenate([value * head_mask(h, BF16) for h in range(HEADS)], axis=0)


def gather_heads(stacked):
    total = stacked[:WT]
    lane = lax.broadcasted_iota(jnp.int32, (1, C), 1)
    for h in range(1, HEADS):
        total = jnp.where(lane >= h * HEAD, stacked[h * WT : (h + 1) * WT], total)
    return total


def window_forward(w, x, gain, wq, wk, wv, bias, extra, save):
    unit_s, inv_s, normed_s, q_s, k_s, v_s, p_s, att_s, s_s, d_s = save
    rows = pl.ds(w * WT, WT)
    xf = x.astype(F32)
    center = xf - jnp.mean(xf, axis=-1, keepdims=True)
    inv = lax.rsqrt(jnp.mean(center * center, axis=-1, keepdims=True) + 1e-05)
    unit = center * inv
    normed = (unit * gain).astype(BF16)
    unit_s[rows, :] = unit
    inv_s[rows, :] = inv
    normed_s[rows, :] = normed
    q = (nn(normed, wq) * FACTOR).astype(BF16)
    k = nn(normed, wk).astype(BF16)
    v = nn(normed, wv).astype(BF16)
    q_s[rows, :] = q
    k_s[rows, :] = k
    v_s[rows, :] = v
    s_s[w] = nt(spread(q), k)
    for at in range(0, HEADS * WT, STEP):
        h, first = at // WT, at % WT
        s = s_s[w, at : at + STEP, :] + bias[h, first : first + STEP, :]
        if extra is not None:
            s = s + extra[first : first + STEP]
        e = jnp.exp(s - jnp.max(s, axis=-1, keepdims=True))
        p = (e * (1.0 / jnp.sum(e, axis=-1, keepdims=True))).astype(BF16)
        p_s[w, at : at + STEP, :] = p
    att = gather_heads(nn(p_s[w], v)).astype(BF16)
    att_s[rows, :] = att
    return xf, att


def window_backward(w, first_one, g, gain, wq, wk, wv, wo, save, grads):
    unit_s, inv_s, normed_s, q_s, k_s, v_s, p_s, att_s, s_s, d_s = save
    gq_s, gk_s, gv_s, go_s, gb_s, gg_s = grads
    rows = pl.ds(w * WT, WT)

    def add(ref, index, value):
        ref[index] = value if first_one else ref[index] + value

    add(go_s, ..., tn(att_s[rows, :], g))
    da = spread(nt(g, wo).astype(BF16))
    s_s[w] = nt(da, v_s[rows, :])
    dv = tn(p_s[w], da).astype(BF16)
    for at in range(0, HEADS * WT, STEP):
        h, first = at // WT, at % WT
        pf = p_s[w, at : at + STEP, :].astype(F32)
        t = pf * s_s[w, at : at + STEP, :]
        ds = t - pf * jnp.sum(t, axis=-1, keepdims=True)
        add(gb_s, (h, slice(first, first + STEP), slice(None)), ds)
        d_s[w, at : at + STEP, :] = ds.astype(BF16)
    ds = d_s[w]
    dk = tn(ds, spread(q_s[rows, :])).astype(BF16)
    dq = (gather_heads(nn(ds, k_s[rows, :])) * FACTOR).astype(BF16)
    normed = normed_s[rows, :]
    add(gq_s, ..., tn(normed, dq))
    add(gk_s, ..., tn(normed, dk))
    add(gv_s, ..., tn(normed, dv))
    dn = nt(dq, wq) + nt(dk, wk) + nt(dv, wv)
    unit = unit_s[rows, :]
    add(gg_s, ..., jnp.sum(dn * unit, axis=0, keepdims=True))
    dh = dn * gain
    d_in = g.astype(F32) + inv_s[rows, :] * (
        dh
        - jnp.mean(dh, axis=-1, keepdims=True)
        - unit * jnp.mean(dh * unit, axis=-1, keepdims=True)
    )
    return d_in.astype(BF16)


def pack(out, grads):
    gq_s, gk_s, gv_s, go_s, gb_s, gg_s = grads
    at = 0

    def put(value):
        nonlocal at
        value = value.astype(BF16)
        done = 0
        while done < value.shape[0]:
            piece, first = (at + done) // PIECE, (at + done) % PIECE
            count = min(PIECE - first, value.shape[0] - done)
            out[piece // SPOTS, piece % SPOTS, first : first + count, :] = value[done : done + count]
            done += count
        at += value.shape[0]

    for ref in (gq_s, gk_s, gv_s, go_s):
        put(ref[:, :128])
    for one, two in ((gq_s, gk_s), (gv_s, go_s)):
        put(jnp.concatenate([one[:, 128:], two[:, 128:]], axis=1))
    for h in range(HEADS):
        put(gb_s[h, :, :128])
    tails = [gb_s[h, :, 128:] for h in range(HEADS)] + [jnp.zeros((WT, 32), F32)]
    put(jnp.concatenate(tails, axis=1))
    gg = gg_s[...]
    second = jnp.concatenate([gg[:, 128:], jnp.zeros((1, 64), F32)], axis=1)
    put(jnp.concatenate([gg[:, :128], second, jnp.zeros((14, 128), F32)], axis=0))
    put(jnp.zeros((2 * HALF - at, 128), F32))


class Sum:
    def __init__(self, lon_count, refs):
        self.in_ref, self.out_ref, self.core_s, self.part_s, self.plane_s, self.line_s = refs[:6]
        self.sems = refs[6:]
        rep, lat = lax.axis_index("rep"), lax.axis_index("lat")
        self.lon = lax.axis_index("lon")
        self.lons = lon_count
        self.core = rep % 2
        x_hi, x_lo, y = rep // 2, lat // 4, lat % 4
        self.me = (x_hi * 2 + x_lo) * 4 + y
        self.partner = {"rep": x_hi * 2 + (1 - self.core)}

    def spot(self, k):
        index = lax.rem(self.me + k, SPOTS)
        x, y = index // 4, index % 4
        return {"rep": (x // 2) * 2 + self.core, "lat": (x % 2) * 4 + y}

    def neighbour(self, k):
        return {"lon": lax.rem(self.lon + k, self.lons)}

    def greet(self, barrier):
        pl.semaphore_signal(barrier, inc=1, device_id=self.partner, device_id_type=MESH)

        def greet_plane(k, carry):
            pl.semaphore_signal(barrier, inc=1, device_id=self.spot(k), device_id_type=MESH)
            return carry

        def greet_line(k, carry):
            pl.semaphore_signal(barrier, inc=1, device_id=self.neighbour(k), device_id_type=MESH)
            return carry

        lax.fori_loop(1, SPOTS, greet_plane, 0)
        lax.fori_loop(1, self.lons, greet_line, 0)
        return SPOTS + self.lons - 1

    def copy(self, pair, k, source, target, device):
        return pltpu.make_async_remote_copy(
            src_ref=source,
            dst_ref=target,
            send_sem=self.sems[2 * pair].at[k],
            recv_sem=self.sems[2 * pair + 1].at[k],
            device_id=device,
            device_id_type=MESH,
        )

    def core_copy(self, k):
        j = lax.rem(self.me + k, SPOTS)
        return self.copy(0, k, self.in_ref.at[1 - self.core, j], self.core_s.at[k], self.partner)

    def plane_copy(self, k):
        return self.copy(1, k, self.part_s.at[k], self.plane_s.at[k], self.spot(k))

    def line_copy(self, k, slot):
        return self.copy(2, k, self.line_s.at[slot], self.line_s.at[slot], self.neighbour(k))

    def back_copy(self, k, j):
        ref = self.out_ref.at[self.core, j]
        return self.copy(3, k, ref, ref, self.spot(k))

    def last_copy(self, k, half):
        ref = self.out_ref.at[half, lax.rem(self.me + SPOTS - k, SPOTS)]
        return self.copy(4, k, ref, ref, self.partner)

    def merge(self, k):
        self.core_copy(k).wait()
        j = lax.rem(self.me + k, SPOTS)
        return self.in_ref[self.core, j].astype(F32) + self.core_s[k].astype(F32)

    def loop(self, first, last, step):
        def body(k, carry):
            step(k)
            return carry

        lax.fori_loop(first, last, body, 0)

    def start_core(self):
        self.loop(1, SPOTS, lambda k: self.core_copy(k).start())
        self.core_copy(0).start()

    def start_plane(self):
        def step(k):
            self.part_s[k] = self.merge(k).astype(BF16)
            self.plane_copy(k).start()

        self.loop(1, SPOTS, step)

    def start_line(self):
        def add(k, total):
            self.plane_copy(k).wait()
            return total + self.plane_s[k].astype(F32)

        total = lax.fori_loop(1, SPOTS, add, self.merge(0))
        self.line_s[self.lon] = total.astype(BF16)
        self.loop(1, self.lons, lambda k: self.line_copy(k, self.lon).start())

    def start_back(self):
        def wait(k):
            self.line_copy(k, self.lon).wait_send()
            self.line_copy(k, lax.rem(self.lon + self.lons - k, self.lons)).wait_recv()

        self.loop(1, self.lons, wait)
        total = self.line_s[0].astype(F32)
        for n in range(1, self.lons):
            total = total + self.line_s[n].astype(F32)
        self.out_ref[self.core, self.me] = total.astype(BF16)
        self.loop(1, SPOTS, lambda k: self.back_copy(k, self.me).start())
        self.last_copy(0, self.core).start()

    def start_last(self):
        def step(k):
            self.back_copy(k, self.me).wait_send()
            self.back_copy(k, lax.rem(self.me + SPOTS - k, SPOTS)).wait_recv()
            self.last_copy(k, self.core).start()

        self.loop(1, SPOTS, step)

    def finish(self):
        def step(k):
            self.last_copy(k, self.core).wait_send()
            self.last_copy(k, 1 - self.core).wait_recv()

        self.loop(0, SPOTS, step)


def layer_kernel(
    lats,
    lons,
    make_sum,
    tok_ref,
    cot_ref,
    gain_a,
    qkv_a,
    out_a,
    bias_a,
    gain_b,
    qkv_b,
    out_b,
    bias_b,
    route_ref,
    dtok_ref,
    sum_ref,
    save_a,
    save_b,
    grad_a,
    grad_b,
    order_s,
    slots_s,
    ahead_s,
    place_s,
    back_s,
    home_s,
    extra_s,
    x_a,
    mid_s,
    dmid_s,
    send_s,
    recv_s,
    send_sem,
    recv_sem,
    packed_s,
    parts_a,
    parts_b,
):
    lat = lax.axis_index("lat")
    lon = lax.axis_index("lon")

    def shifted(dlat, dlon):
        return {"lat": lax.rem(lat + dlat + lats, lats), "lon": lax.rem(lon + dlon + lons, lons)}

    before = [shifted(0, -1), shifted(-1, 0), shifted(-1, -1)]
    after = [shifted(0, 1), shifted(1, 0), shifted(1, 1)]

    def quarters(leg, window):
        copies = []
        for n, target in enumerate(after if leg == 2 else before):
            at = (leg, n + 1) if window is None else (leg, n + 1, window)
            sem = n if window is None else 3 + (leg - 1) * 12 + window * 3 + n
            copies.append(
                pltpu.make_async_remote_copy(
                    src_ref=send_s.at[at],
                    dst_ref=recv_s.at[at],
                    send_sem=send_sem.at[sem],
                    recv_sem=recv_sem.at[sem],
                    device_id=target,
                    device_id_type=MESH,
                )
            )
        return copies

    def post(leg, window, value):
        value = value.astype(BF16)
        recv_s[leg, 0, window] = value[:SLOT]
        for n in range(1, 4):
            send_s[leg, n, window] = value[n * SLOT : (n + 1) * SLOT]
        copies = quarters(leg, window)
        for copy in copies:
            copy.start()
        return copies

    def arrived(leg, window):
        return recv_s[leg, :, window].reshape(4 * SLOT, C)

    sum_a = make_sum(lons, (packed_s.at[0], sum_ref.at[0]) + parts_a)
    sum_b = make_sum(lons, (packed_s.at[1], sum_ref.at[1]) + parts_b)

    barrier = pltpu.get_barrier_semaphore()
    for other in before + after:
        pl.semaphore_signal(barrier, inc=1, device_id=other, device_id_type=MESH)
    greeted = 6 + sum_a.greet(barrier)

    def one_hot(rows, row, columns):
        target = route_ref[row : row + 1, :columns]
        spot = lax.broadcasted_iota(jnp.int32, (rows, columns), 0)
        return jnp.where(spot == target, 1.0, 0.0).astype(BF16)

    x_a[...] = nn(one_hot(TOK, 0, TOK), tok_ref[...]).astype(BF16)
    order_s[...] = one_hot(TOK, 1, TOK)
    slots_s[...] = one_hot(16 * SLOT, 2, TOK)
    place_s[...] = one_hot(WT, 5, 4 * SLOT)
    back_s[...] = one_hot(4 * SLOT, 6, WT)
    for n in range(2):
        ahead_s[n] = one_hot(4 * SLOT, 3 + n, 72)
        home_s[n] = one_hot(72, 7 + n, 4 * SLOT)

    ga = gain_a[...]
    wo = out_a[...]
    wqa, wka, wva = (qkv_a[:, n * C : (n + 1) * C] for n in range(3))
    mids = [None] * WINDOWS
    backs = [None] * WINDOWS

    def send_mid(w):
        levels = (2 * w + 1, (2 * w + 2) % LEVELS)
        mids[w] = post(1, w, nn(ahead_s[0], mid_s[levels[0]]) + nn(ahead_s[1], mid_s[levels[1]]))

    for w in range(WINDOWS):
        xf, att = window_forward(w, x_a[w * WT : (w + 1) * WT, :], ga, wqa, wka, wva, bias_a, None, save_a)
        middle = xf + nn(att, wo)
        mid_s[2 * w] = middle[:72].astype(BF16)
        mid_s[2 * w + 1] = middle[72:].astype(BF16)
        if w == 0:
            cots = nn(slots_s[...], cot_ref[...]).astype(BF16)
            cots = cots.reshape(4, WINDOWS, SLOT, C)
            recv_s[0, 0] = cots[0]
            for n in range(1, 4):
                send_s[0, n] = cots[n]
            pl.semaphore_wait(barrier, greeted)
            cot_copies = quarters(0, None)
            for copy in cot_copies:
                copy.start()
        else:
            send_mid(w - 1)
    send_mid(WINDOWS - 1)

    def label(shape, axis, level):
        at = lax.broadcasted_iota(jnp.int32, shape, axis)
        upper = jnp.where(at >= 72, 1, 0)
        inside = at - 72 * upper
        late = jnp.where(inside >= 36, 1, 0) * jnp.where(lat == lats - 1, 1, 0)
        return late + 2 * upper if level else late

    for n in range(2):
        same = label((WT, WT), 0, n) == label((WT, WT), 1, n)
        extra_s[n] = jnp.where(same, 0.0, -1e30)

    gb = gain_b[...]
    wob = out_b[...]
    wqb, wkb, wvb = (qkv_b[:, n * C : (n + 1) * C] for n in range(3))

    for copy in cot_copies:
        copy.wait()
    for w in range(WINDOWS):
        for copy in mids[w]:
            copy.wait()
        x = nn(place_s[...], arrived(1, w)).astype(BF16)
        g = nn(place_s[...], arrived(0, w)).astype(BF16)
        window_forward(w, x, gb, wqb, wkb, wvb, bias_b, extra_s.at[w // (WINDOWS - 1)], save_b)
        d_in = window_backward(w, w == 0, g, gb, wqb, wkb, wvb, wob, save_b, grad_b)
        backs[w] = post(2, w, nn(back_s[...], d_in))

    pack(packed_s.at[1], grad_b)
    sum_b.start_core()

    def take_back(w):
        for copy in backs[w]:
            copy.wait()
        value = arrived(2, w)
        dmid_s[2 * w + 1] = nn(home_s[0], value)
        dmid_s[(2 * w + 2) % LEVELS] = nn(home_s[1], value)

    def regular_back(w, first_one):
        g = jnp.concatenate([dmid_s[2 * w], dmid_s[2 * w + 1]], axis=0).astype(BF16)
        x_a[w * WT : (w + 1) * WT, :] = window_backward(
            w, first_one, g, ga, wqa, wka, wva, wo, save_a, grad_a
        )

    take_back(0)
    take_back(1)
    regular_back(1, True)
    sum_b.start_plane()
    take_back(2)
    regular_back(2, False)
    take_back(3)
    regular_back(3, False)
    regular_back(0, False)
    pack(packed_s.at[0], grad_a)
    sum_a.start_core()
    dtok_ref[...] = nn(order_s[...], x_a[...]).astype(BF16)
    sum_a.start_plane()
    sum_b.start_line()
    sum_b.start_back()
    sum_a.start_line()
    sum_b.start_last()
    sum_a.start_back()
    sum_a.start_last()
    sum_b.finish()
    sum_a.finish()


def unpack_kernel(in_ref, dtok_ref, dtok_out, *outs):
    dtok_out[...] = dtok_ref[...]
    for block in range(2):
        gain, qkv, out, bias = outs[4 * block : 4 * block + 4]
        at = block * 2 * HALF

        def rows(count):
            nonlocal at
            at += count
            return in_ref[at - count : at, :].astype(F32)

        gq, gk, gv, go = (rows(C) for _ in range(4))
        one, two = rows(C), rows(C)
        qkv[...] = jnp.concatenate(
            [gq, one[:, :64], gk, one[:, 64:], gv, two[:, :64]], axis=1
        )
        out[...] = jnp.concatenate([go, two[:, 64:]], axis=1)
        main = [rows(WT) for _ in range(HEADS)]
        tails = rows(WT)
        for h in range(HEADS):
            bias[h] = jnp.concatenate([main[h], tails[:, 16 * h : 16 * h + 16]], axis=1)
        last = rows(16)
        gain[...] = jnp.concatenate([last[0:1, :], last[1:2, :64]], axis=1)


def saves():
    return (
        pltpu.VMEM((TOK, C), F32),
        pltpu.VMEM((TOK, 1), F32),
        pltpu.VMEM((TOK, C), BF16),
        pltpu.VMEM((TOK, C), BF16),
        pltpu.VMEM((TOK, C), BF16),
        pltpu.VMEM((TOK, C), BF16),
        pltpu.VMEM((WINDOWS, HEADS * WT, WT), BF16),
        pltpu.VMEM((TOK, C), BF16),
        pltpu.VMEM((WINDOWS, HEADS * WT, WT), F32),
        pltpu.VMEM((WINDOWS, HEADS * WT, WT), BF16),
    )


def totals():
    return (
        pltpu.VMEM((C, C), F32),
        pltpu.VMEM((C, C), F32),
        pltpu.VMEM((C, C), F32),
        pltpu.VMEM((C, C), F32),
        pltpu.VMEM((HEADS, WT, WT), F32),
        pltpu.VMEM((1, C), F32),
    )


def parts(lons):
    piece = (PIECE, 128)
    return (
        (pltpu.VMEM((SPOTS,) + piece, BF16),) * 3
        + (pltpu.VMEM((lons,) + piece, BF16),)
        + (pltpu.SemaphoreType.DMA((SPOTS,)),) * 4
        + (pltpu.SemaphoreType.DMA((lons,)),) * 2
        + (pltpu.SemaphoreType.DMA((SPOTS,)),) * 4
    )


def run_layer(lats, lons, *args):
    return pl.pallas_call(
        functools.partial(layer_kernel, lats, lons, Sum),
        out_shape=(
            jax.ShapeDtypeStruct((TOK, C), BF16),
            jax.ShapeDtypeStruct((2, 2, SPOTS, PIECE, 128), BF16),
        ),
        in_specs=[pl.BlockSpec(memory_space=pltpu.VMEM)] * 11,
        out_specs=(pl.BlockSpec(memory_space=pltpu.VMEM),) * 2,
        scratch_shapes=[
            saves(),
            saves(),
            totals(),
            totals(),
            pltpu.VMEM((TOK, TOK), BF16),
            pltpu.VMEM((16 * SLOT, TOK), BF16),
            pltpu.VMEM((2, 4 * SLOT, 72), BF16),
            pltpu.VMEM((WT, 4 * SLOT), BF16),
            pltpu.VMEM((4 * SLOT, WT), BF16),
            pltpu.VMEM((2, 72, 4 * SLOT), BF16),
            pltpu.VMEM((2, WT, WT), F32),
            pltpu.VMEM((TOK, C), BF16),
            pltpu.VMEM((LEVELS, 72, C), BF16),
            pltpu.VMEM((LEVELS, 72, C), F32),
            pltpu.VMEM((3, 4, WINDOWS, SLOT, C), BF16),
            pltpu.VMEM((3, 4, WINDOWS, SLOT, C), BF16),
            pltpu.SemaphoreType.DMA((27,)),
            pltpu.SemaphoreType.DMA((27,)),
            pltpu.VMEM((2, 2, SPOTS, PIECE, 128), BF16),
            parts(lons),
            parts(lons),
        ],
        compiler_params=pltpu.CompilerParams(
            collective_id=0, has_side_effects=True, vmem_limit_bytes=VMEM_LIMIT
        ),
        name="layer",
    )(*args)


def run_unpack(summed, d_tokens):
    block = (
        jax.ShapeDtypeStruct((1, C), F32),
        jax.ShapeDtypeStruct((C, 3 * C), F32),
        jax.ShapeDtypeStruct((C, C), F32),
        jax.ShapeDtypeStruct((HEADS, WT, WT), F32),
    )
    return pl.pallas_call(
        unpack_kernel,
        out_shape=(jax.ShapeDtypeStruct((TOK, C), BF16),) + block + block,
        in_specs=[pl.BlockSpec(memory_space=pltpu.VMEM)] * 2,
        out_specs=(pl.BlockSpec(memory_space=pltpu.VMEM),) * 9,
        compiler_params=pltpu.CompilerParams(vmem_limit_bytes=VMEM_LIMIT),
        name="unpack",
    )(summed, d_tokens)


def solution(mesh):
    lats, lons = mesh.shape["lat"], mesh.shape["lon"]
    route = routes()

    def stored(grid):
        return grid.transpose(0, 2, 3, 1, 4).reshape(TOK, C)

    def local(tokens, cotangent, gain_a, qkv_a, out_a, bias_a, gain_b, qkv_b, out_b, bias_b):
        d_tokens, summed = run_layer(
            lats,
            lons,
            stored(tokens),
            stored(cotangent),
            gain_a.reshape(1, C),
            qkv_a,
            out_a,
            bias_a,
            gain_b.reshape(1, C),
            qkv_b,
            out_b,
            bias_b,
            jnp.asarray(route),
        )
        d_tokens, ga, qa, oa, ba, gb, qb, ob, bb = run_unpack(
            summed.reshape(4 * HALF, 128), d_tokens
        )
        d_tokens = d_tokens.reshape(1, 6, 12, LEVELS, C).transpose(0, 3, 1, 2, 4)
        return (
            d_tokens,
            ga.reshape(C),
            qa,
            oa,
            ba,
            gb.reshape(C),
            qb,
            ob,
            bb,
        )

    grid = P("rep", None, "lat", "lon", None)
    return jax.shard_map(
        local,
        mesh=mesh,
        in_specs=(grid, grid) + (P(),) * 8,
        out_specs=(grid,) + (P(),) * 8,
        check_vma=False,
    )
```

time: 100 us -> 74.6 us (0.75)
  Pallas kernels: 93.9 us -> 73.8 us
  local copies, waits for them, and re-layouts: 5.25 us -> 0 us
    pallas_call x3 -> x2, Pallas kernels: 93.9 us -> 73.8 us  [the longest x1 70.5 us: run_layer(): pl.pallas_call(functools.partial(layer_kernel, lats, lons, Sum), out_shap...]
    unnamed x21 -> x0, local copies, waits for them, and re-layouts: 3.9 us -> none
    reshape x3 -> x0, local copies, waits for them, and re-layouts: 1.35 us -> none  [the longest x1 1.13 us: local(): cotangent.reshape(TOK, C)]
where the time goes in v2:
time: 74.6 us; the launch traced here: 74.5 us
  Pallas kernels  73.8 us (99%)
    pallas_call x1, Pallas kernels, run_layer(): pl.pallas_call(functools.partial(layer_kernel, lats, lons, Sum), out_shap...  70.5 us
    pallas_call x1, Pallas kernels, run_unpack(): pl.pallas_call(unpack_kernel, out_shape=(jax.ShapeDtypeStruct((TOK, C), B...  3.28 us

profile of v2, /device:TPU:1, one launch (start us, length us, event | category | flops | bytes accessed | tf_op | source)
XLA Modules:
  0.0 74.5 jit_solution(2137009212065737860)
XLA Ops:
  0.6 70.5 %layer.1 = (bf16[576,192]{1,0:T(8,128)(2,1)}, bf16[2,2,16,80,128]{4,3,2,1,0:T(8,128)(2,1)}) custom-call(bf16[576,192]{1,0:T(8,128)(2,1)} %bitcast.15, bf16[576,192]{1,0:T(8,128)(2,1)} %bitcast.16, f32[1,192]{1,0:T(1,128)} %bitcast.17, bf16[192,576]{1,0:T(8,128)(2,1)} %qkv_a.1, bf16[192,192]{1,0:T(8,128)(2,1)} %out_a.1, f32[6,144,144]{2,1,0:T(8,128)} %bias_a.1, ...), custom_call_target="tpu_custom_call" | custom-call | tf_op jit(solution)/shard_map/layer/pallas_call | solution.py:562
  71.2 3.3 %unpack.1 = (bf16[576,192]{1,0:T(8,128)(2,1)}, f32[1,192]{1,0:T(1,128)}, f32[192,576]{1,0:T(8,128)}, f32[192,192]{1,0:T(8,128)}, f32[6,144,144]{2,1,0:T(8,128)},...) custom-call(bf16[5120,128]{1,0:T(8,128)(2,1)} %bitcast.14, ...), custom_call_target="tpu_custom_call" | custom-call | tf_op jit(solution)/shard_map/unpack/pallas_call | solution.py:607

commit v3 on v2

--- a/solution.py
+++ b/solution.py
@@ -23,8 +23,10 @@
 SPOTS = 16
 HALF = PIECE * SPOTS
 STEP = 144
+GROUPS = ((0, 4, 0, 128), (4, 6, 128, 192))
+LOG2E = 1.4426950408889634
 SLOT = 48
-VMEM_LIMIT = 56 * 1024 * 1024
+VMEM_LIMIT = 40 * 1024 * 1024
 
 
 def nt(left, right):
@@ -69,19 +71,31 @@
 
 
 def spread(value):
-    return jnp.concatenate([value * head_mask(h, BF16) for h in range(HEADS)], axis=0)
+    return [
+        jnp.concatenate(
+            [value[:, lo:hi] * head_mask(h, BF16)[:, lo:hi] for h in range(first, last)], axis=0
+        )
+        for first, last, lo, hi in GROUPS
+    ]
 
 
 def gather_heads(stacked):
-    total = stacked[:WT]
-    lane = lax.broadcasted_iota(jnp.int32, (1, C), 1)
-    for h in range(1, HEADS):
-        total = jnp.where(lane >= h * HEAD, stacked[h * WT : (h + 1) * WT], total)
-    return total
+    parts = []
+    for group, (first, last, lo, hi) in zip(stacked, GROUPS):
+        lane = lax.broadcasted_iota(jnp.int32, (1, hi - lo), 1)
+        total = group[:WT]
+        for n in range(1, last - first):
+            total = jnp.where(lane >= n * HEAD, group[n * WT : (n + 1) * WT], total)
+        parts.append(total)
+    return jnp.concatenate(parts, axis=1)
+
+
+def stacked_rows(first, last):
+    return slice(first * WT, last * WT)
 
 
 def window_forward(w, x, gain, wq, wk, wv, bias, extra, save):
-    unit_s, inv_s, normed_s, q_s, k_s, v_s, p_s, att_s, s_s, d_s = save
+    (unit_s, inv_s, normed_s, q_s, k_s, v_s, p_s, att_s), (s_s, d_s) = save
     rows = pl.ds(w * WT, WT)
     xf = x.astype(F32)
     center = xf - jnp.mean(xf, axis=-1, keepdims=True)
@@ -91,28 +105,31 @@
     unit_s[rows, :] = unit
     inv_s[rows, :] = inv
     normed_s[rows, :] = normed
-    q = (nn(normed, wq) * FACTOR).astype(BF16)
+    q = (nn(normed, wq) * (FACTOR * LOG2E)).astype(BF16)
     k = nn(normed, wk).astype(BF16)
     v = nn(normed, wv).astype(BF16)
     q_s[rows, :] = q
     k_s[rows, :] = k
     v_s[rows, :] = v
-    s_s[w] = nt(spread(q), k)
+    for left, (head, stop, lo, hi) in zip(spread(q), GROUPS):
+        s_s[w, stacked_rows(head, stop), :] = nt(left, k[:, lo:hi])
     for at in range(0, HEADS * WT, STEP):
         h, first = at // WT, at % WT
         s = s_s[w, at : at + STEP, :] + bias[h, first : first + STEP, :]
         if extra is not None:
             s = s + extra[first : first + STEP]
-        e = jnp.exp(s - jnp.max(s, axis=-1, keepdims=True))
+        e = jnp.exp2(s - jnp.max(s, axis=-1, keepdims=True))
         p = (e * (1.0 / jnp.sum(e, axis=-1, keepdims=True))).astype(BF16)
         p_s[w, at : at + STEP, :] = p
-    att = gather_heads(nn(p_s[w], v)).astype(BF16)
+    att = gather_heads(
+        [nn(p_s[w, stacked_rows(head, stop), :], v[:, lo:hi]) for head, stop, lo, hi in GROUPS]
+    ).astype(BF16)
     att_s[rows, :] = att
     return xf, att
 
 
 def window_backward(w, first_one, g, gain, wq, wk, wv, wo, save, grads):
-    unit_s, inv_s, normed_s, q_s, k_s, v_s, p_s, att_s, s_s, d_s = save
+    (unit_s, inv_s, normed_s, q_s, k_s, v_s, p_s, att_s), (s_s, d_s) = save
     gq_s, gk_s, gv_s, go_s, gb_s, gg_s = grads
     rows = pl.ds(w * WT, WT)
 
@@ -121,8 +138,13 @@
 
     add(go_s, ..., tn(att_s[rows, :], g))
     da = spread(nt(g, wo).astype(BF16))
-    s_s[w] = nt(da, v_s[rows, :])
-    dv = tn(p_s[w], da).astype(BF16)
+    v = v_s[rows, :]
+    k = k_s[rows, :]
+    dvs = []
+    for left, (head, stop, lo, hi) in zip(da, GROUPS):
+        s_s[w, stacked_rows(head, stop), :] = nt(left, v[:, lo:hi])
+        dvs.append(tn(p_s[w, stacked_rows(head, stop), :], left))
+    dv = jnp.concatenate(dvs, axis=1).astype(BF16)
     for at in range(0, HEADS * WT, STEP):
         h, first = at // WT, at % WT
         pf = p_s[w, at : at + STEP, :].astype(F32)
@@ -130,9 +152,13 @@
         ds = t - pf * jnp.sum(t, axis=-1, keepdims=True)
         add(gb_s, (h, slice(first, first + STEP), slice(None)), ds)
         d_s[w, at : at + STEP, :] = ds.astype(BF16)
-    ds = d_s[w]
-    dk = tn(ds, spread(q_s[rows, :])).astype(BF16)
-    dq = (gather_heads(nn(ds, k_s[rows, :])) * FACTOR).astype(BF16)
+    dks, dqs = [], []
+    for left, (head, stop, lo, hi) in zip(spread(q_s[rows, :]), GROUPS):
+        ds = d_s[w, stacked_rows(head, stop), :]
+        dks.append(tn(ds, left))
+        dqs.append(nn(ds, k[:, lo:hi]))
+    dk = (jnp.concatenate(dks, axis=1) * (1.0 / LOG2E)).astype(BF16)
+    dq = (gather_heads(dqs) * FACTOR).astype(BF16)
     normed = normed_s[rows, :]
     add(gq_s, ..., tn(normed, dq))
     add(gk_s, ..., tn(normed, dk))
@@ -319,6 +345,8 @@
     route_ref,
     dtok_ref,
     sum_ref,
+    scaled_s,
+    room,
     save_a,
     save_b,
     grad_a,
@@ -343,6 +371,7 @@
 ):
     lat = lax.axis_index("lat")
     lon = lax.axis_index("lon")
+    save_a, save_b = (save_a, room), (save_b, room)
 
     def shifted(dlat, dlon):
         return {"lat": lax.rem(lat + dlat + lats, lats), "lon": lax.rem(lon + dlon + lons, lons)}
@@ -394,13 +423,10 @@
         return jnp.where(spot == target, 1.0, 0.0).astype(BF16)
 
     x_a[...] = nn(one_hot(TOK, 0, TOK), tok_ref[...]).astype(BF16)
-    order_s[...] = one_hot(TOK, 1, TOK)
+    scaled_s[0] = bias_a[...] * LOG2E
     slots_s[...] = one_hot(16 * SLOT, 2, TOK)
-    place_s[...] = one_hot(WT, 5, 4 * SLOT)
-    back_s[...] = one_hot(4 * SLOT, 6, WT)
     for n in range(2):
         ahead_s[n] = one_hot(4 * SLOT, 3 + n, 72)
-        home_s[n] = one_hot(72, 7 + n, 4 * SLOT)
 
     ga = gain_a[...]
     wo = out_a[...]
@@ -413,7 +439,7 @@
         mids[w] = post(1, w, nn(ahead_s[0], mid_s[levels[0]]) + nn(ahead_s[1], mid_s[levels[1]]))
 
     for w in range(WINDOWS):
-        xf, att = window_forward(w, x_a[w * WT : (w + 1) * WT, :], ga, wqa, wka, wva, bias_a, None, save_a)
+        xf, att = window_forward(w, x_a[w * WT : (w + 1) * WT, :], ga, wqa, wka, wva, scaled_s.at[0], None, save_a)
         middle = xf + nn(att, wo)
         mid_s[2 * w] = middle[:72].astype(BF16)
         mid_s[2 * w + 1] = middle[72:].astype(BF16)
@@ -423,13 +449,21 @@
             recv_s[0, 0] = cots[0]
             for n in range(1, 4):
                 send_s[0, n] = cots[n]
-            pl.semaphore_wait(barrier, greeted)
-            cot_copies = quarters(0, None)
-            for copy in cot_copies:
-                copy.start()
         else:
+            if w == 1:
+                pl.semaphore_wait(barrier, greeted)
+                cot_copies = quarters(0, None)
+                for copy in cot_copies:
+                    copy.start()
             send_mid(w - 1)
     send_mid(WINDOWS - 1)
+
+    order_s[...] = one_hot(TOK, 1, TOK)
+    place_s[...] = one_hot(WT, 5, 4 * SLOT)
+    back_s[...] = one_hot(4 * SLOT, 6, WT)
+    for n in range(2):
+        home_s[n] = one_hot(72, 7 + n, 4 * SLOT)
+    scaled_s[1] = bias_b[...] * LOG2E
 
     def label(shape, axis, level):
         at = lax.broadcasted_iota(jnp.int32, shape, axis)
@@ -453,7 +487,7 @@
             copy.wait()
         x = nn(place_s[...], arrived(1, w)).astype(BF16)
         g = nn(place_s[...], arrived(0, w)).astype(BF16)
-        window_forward(w, x, gb, wqb, wkb, wvb, bias_b, extra_s.at[w // (WINDOWS - 1)], save_b)
+        window_forward(w, x, gb, wqb, wkb, wvb, scaled_s.at[1], extra_s.at[w // (WINDOWS - 1)], save_b)
         d_in = window_backward(w, w == 0, g, gb, wqb, wkb, wvb, wob, save_b, grad_b)
         backs[w] = post(2, w, nn(back_s[...], d_in))
 
@@ -531,6 +565,11 @@
         pltpu.VMEM((TOK, C), BF16),
         pltpu.VMEM((WINDOWS, HEADS * WT, WT), BF16),
         pltpu.VMEM((TOK, C), BF16),
+    )
+
+
+def rooms():
+    return (
         pltpu.VMEM((WINDOWS, HEADS * WT, WT), F32),
         pltpu.VMEM((WINDOWS, HEADS * WT, WT), BF16),
     )
@@ -568,6 +607,8 @@
         in_specs=[pl.BlockSpec(memory_space=pltpu.VMEM)] * 11,
         out_specs=(pl.BlockSpec(memory_space=pltpu.VMEM),) * 2,
         scratch_shapes=[
+            pltpu.VMEM((2, HEADS, WT, WT), F32),
+            rooms(),
             saves(),
             saves(),
             totals(),

time: 74.6 us -> 79.7 us (1.068)
  local copies, waits for them, and re-layouts: 0 us -> 10.1 us
  Pallas kernels: 73.8 us -> 68.6 us
    unnamed x0 -> x22, local copies, waits for them, and re-layouts: none -> 10.1 us
    pallas_call x1, Pallas kernels: 70.5 us -> 66.6 us  [run_layer(): pl.pallas_call(functools.partial(layer_kernel, lats, lons, Sum), out_shap...]
    pallas_call x1, Pallas kernels: 3.28 us -> 1.93 us  [run_unpack(): pl.pallas_call(unpack_kernel, out_shape=(jax.ShapeDtypeStruct((TOK, C), B...]
where the time goes in v3:
time: 79.7 us; the launch traced here: 79.3 us
  Pallas kernels  68.6 us (86%)
  local copies, waits for them, and re-layouts  10.1 us (13%)
    pallas_call x1, Pallas kernels, run_layer(): pl.pallas_call(functools.partial(layer_kernel, lats, lons, Sum), out_shap...  66.6 us
    unnamed x22, local copies, waits for them, and re-layouts  10.1 us
    pallas_call x1, Pallas kernels, run_unpack(): pl.pallas_call(unpack_kernel, out_shape=(jax.ShapeDtypeStruct((TOK, C), B...  1.93 us

profile of v3, /device:TPU:1, one launch (start us, length us, event | category | flops | bytes accessed | tf_op | source)
XLA Modules:
  0.0 79.3 jit_solution(15244602569635476294)
XLA Ops:
  0.6 0.0 copy-start
  0.7 1.2 %copy-done = f32[6,144,144]{2,1,0:T(8,128)S(1)} copy-done((f32[6,144,144]{2,1,0:T(8,128)S(1)}, f32[6,144,144]{2,1,0:T(8,128)}, u32[]{:S(2)}) %copy-start) | copy-done | bytes 497688
  1.8 0.0 copy-start.1
  1.8 1.2 %copy-done.1 = f32[6,144,144]{2,1,0:T(8,128)S(1)} copy-done((f32[6,144,144]{2,1,0:T(8,128)S(1)}, f32[6,144,144]{2,1,0:T(8,128)}, u32[]{:S(2)}) %copy-start.1) | copy-done | bytes 497688
  3.0 0.0 copy-start.2
  3.0 1.0 %copy-done.2 = bf16[1,8,6,12,192]{4,1,3,2,0:T(8,128)(2,1)S(1)} copy-done((bf16[1,8,6,12,192]{4,1,3,2,0:T(8,128)(2,1)S(1)}, bf16[1,8,6,12,192]{4,1,3,2,0:T(8,128)(2,1)}, u32[]{:S(2)}) %copy-start.2) | copy-done | bytes 221208
  3.9 0.0 copy-start.3
  3.9 1.0 %copy-done.3 = bf16[1,8,6,12,192]{4,1,3,2,0:T(8,128)(2,1)S(1)} copy-done((bf16[1,8,6,12,192]{4,1,3,2,0:T(8,128)(2,1)S(1)}, bf16[1,8,6,12,192]{4,1,3,2,0:T(8,128)(2,1)}, u32[]{:S(2)}) %copy-start.3) | copy-done | bytes 221208
  4.9 0.0 copy-start.4
  4.9 0.9 %copy-done.4 = bf16[192,576]{1,0:T(8,128)(2,1)S(1)} copy-done((bf16[192,576]{1,0:T(8,128)(2,1)S(1)}, bf16[192,576]{1,0:T(8,128)(2,1)}, u32[]{:S(2)}) %copy-start.4) | copy-done | bytes 221208
  5.9 0.0 copy-start.5
  5.9 0.9 %copy-done.5 = bf16[192,576]{1,0:T(8,128)(2,1)S(1)} copy-done((bf16[192,576]{1,0:T(8,128)(2,1)S(1)}, bf16[192,576]{1,0:T(8,128)(2,1)}, u32[]{:S(2)}) %copy-start.5) | copy-done | bytes 221208
  6.8 0.0 copy-start.6
  6.8 0.9 %copy-done.6 = bf16[192,192]{1,0:T(8,128)(2,1)S(1)} copy-done((bf16[192,192]{1,0:T(8,128)(2,1)S(1)}, bf16[192,192]{1,0:T(8,128)(2,1)}, u32[]{:S(2)}) %copy-start.6) | copy-done | bytes 73752
  7.7 0.0 copy-start.7
  7.7 0.9 %copy-done.7 = bf16[192,192]{1,0:T(8,128)(2,1)S(1)} copy-done((bf16[192,192]{1,0:T(8,128)(2,1)S(1)}, bf16[192,192]{1,0:T(8,128)(2,1)}, u32[]{:S(2)}) %copy-start.7) | copy-done | bytes 73752
  8.6 0.0 copy-start.8
  8.6 0.8 copy-done.8
  9.4 0.0 copy-start.9
  9.4 0.7 copy-done.9
  10.0 0.0 copy-start.10
  10.0 0.7 copy-done.10
  10.7 66.6 %layer.1 = (bf16[576,192]{1,0:T(8,128)(2,1)S(1)}, bf16[2,2,16,80,128]{4,3,2,1,0:T(8,128)(2,1)S(1)}) custom-call(bf16[576,192]{1,0:T(8,128)(2,1)S(1)} %bitcast.15, bf16[576,192]{1,0:T(8,128)(2,1)S(1)} %bitcast.16, f32[1,192]{1,0:T(1,128)S(1)} %bitcast.17, bf16[192,576]{1,0:T(8,128)(2,1)S(1)} %copy-done.4, bf16[192,192]{1,0:T(8,128)(2,1)S(1)} %copy-done.6, ...), custom_call_target="tpu_custom_call" | custom-call | tf_op jit(solution)/shard_map/layer/pallas_call | solution.py:601
  77.4 1.9 %unpack.1 = (bf16[576,192]{1,0:T(8,128)(2,1)}, f32[1,192]{1,0:T(1,128)}, f32[192,576]{1,0:T(8,128)}, f32[192,192]{1,0:T(8,128)}, f32[6,144,144]{2,1,0:T(8,128)},...) custom-call(bf16[5120,128]{1,0:T(8,128)(2,1)S(1)} %bitcast.14, ...), custom_call_target="tpu_custom_call" | custom-call | tf_op jit(solution)/shard_map/unpack/pallas_call | solution.py:648
Async XLA Ops:
  0.6 1.2 %copy-start = (f32[6,144,144]{2,1,0:T(8,128)S(1)}, f32[6,144,144]{2,1,0:T(8,128)}, u32[]{:S(2)}) copy-start(f32[6,144,144]{2,1,0:T(8,128)} %bias_a.1) | copy-start | bytes 1492996
  1.8 1.2 %copy-start.1 = (f32[6,144,144]{2,1,0:T(8,128)S(1)}, f32[6,144,144]{2,1,0:T(8,128)}, u32[]{:S(2)}) copy-start(f32[6,144,144]{2,1,0:T(8,128)} %bias_b.1) | copy-start | bytes 1492996
  3.0 1.0 %copy-start.2 = (bf16[1,8,6,12,192]{4,1,3,2,0:T(8,128)(2,1)S(1)}, bf16[1,8,6,12,192]{4,1,3,2,0:T(8,128)(2,1)}, u32[]{:S(2)}) copy-start(bf16[1,8,6,12,192]{4,1,3,2,0:T(8,128)(2,1)} %param.11) | copy-start | bytes 663556
  3.9 1.0 %copy-start.3 = (bf16[1,8,6,12,192]{4,1,3,2,0:T(8,128)(2,1)S(1)}, bf16[1,8,6,12,192]{4,1,3,2,0:T(8,128)(2,1)}, u32[]{:S(2)}) copy-start(bf16[1,8,6,12,192]{4,1,3,2,0:T(8,128)(2,1)} %param.12) | copy-start | bytes 663556
  4.9 0.9 %copy-start.4 = (bf16[192,576]{1,0:T(8,128)(2,1)S(1)}, bf16[192,576]{1,0:T(8,128)(2,1)}, u32[]{:S(2)}) copy-start(bf16[192,576]{1,0:T(8,128)(2,1)} %qkv_a.1) | copy-start | bytes 663556
  5.9 0.9 %copy-start.5 = (bf16[192,576]{1,0:T(8,128)(2,1)S(1)}, bf16[192,576]{1,0:T(8,128)(2,1)}, u32[]{:S(2)}) copy-start(bf16[192,576]{1,0:T(8,128)(2,1)} %qkv_b.1) | copy-start | bytes 663556
  6.8 0.9 %copy-start.6 = (bf16[192,192]{1,0:T(8,128)(2,1)S(1)}, bf16[192,192]{1,0:T(8,128)(2,1)}, u32[]{:S(2)}) copy-start(bf16[192,192]{1,0:T(8,128)(2,1)} %out_a.1) | copy-start | bytes 221188
  7.7 0.9 %copy-start.7 = (bf16[192,192]{1,0:T(8,128)(2,1)S(1)}, bf16[192,192]{1,0:T(8,128)(2,1)}, u32[]{:S(2)}) copy-start(bf16[192,192]{1,0:T(8,128)(2,1)} %out_b.1) | copy-start | bytes 221188
  8.6 0.8 copy-start.8
  9.4 0.7 copy-start.9
  10.0 0.7 copy-start.10

commit v4 on v3

--- a/solution.py
+++ b/solution.py
@@ -26,7 +26,7 @@
 GROUPS = ((0, 4, 0, 128), (4, 6, 128, 192))
 LOG2E = 1.4426950408889634
 SLOT = 48
-VMEM_LIMIT = 40 * 1024 * 1024
+VMEM_LIMIT = 56 * 1024 * 1024
 
 
 def nt(left, right):
@@ -204,6 +204,15 @@
     put(jnp.zeros((2 * HALF - at, 128), F32))
 
 
+def ring_distance(step, count):
+    return min(step, count - step)
+
+
+FAR_FIRST = sorted(
+    range(1, SPOTS), key=lambda k: -ring_distance(k // 4, 4) - ring_distance(k % 4, 4)
+)
+
+
 class Sum:
     def __init__(self, lon_count, refs):
         self.in_ref, self.out_ref, self.core_s, self.part_s, self.plane_s, self.line_s = refs[:6]
@@ -213,12 +222,19 @@
         self.lons = lon_count
         self.core = rep % 2
         x_hi, x_lo, y = rep // 2, lat // 4, lat % 4
-        self.me = (x_hi * 2 + x_lo) * 4 + y
+        self.x, self.y = x_hi * 2 + x_lo, y
+        self.me = self.x * 4 + y
+        self.far_line = sorted(range(1, lon_count), key=lambda k: -ring_distance(k, lon_count))
         self.partner = {"rep": x_hi * 2 + (1 - self.core)}
 
+    def there(self, k):
+        return lax.rem(self.x + k // 4, 4) * 4 + lax.rem(self.y + k % 4, 4)
+
+    def origin(self, k):
+        return lax.rem(self.x + 4 - k // 4, 4) * 4 + lax.rem(self.y + 4 - k % 4, 4)
+
     def spot(self, k):
-        index = lax.rem(self.me + k, SPOTS)
-        x, y = index // 4, index % 4
+        x, y = lax.rem(self.x + k // 4, 4), lax.rem(self.y + k % 4, 4)
         return {"rep": (x // 2) * 2 + self.core, "lat": (x % 2) * 4 + y}
 
     def neighbour(self, k):
@@ -250,7 +266,7 @@
         )
 
     def core_copy(self, k):
-        j = lax.rem(self.me + k, SPOTS)
+        j = self.there(k)
         return self.copy(0, k, self.in_ref.at[1 - self.core, j], self.core_s.at[k], self.partner)
 
     def plane_copy(self, k):
@@ -264,12 +280,12 @@
         return self.copy(3, k, ref, ref, self.spot(k))
 
     def last_copy(self, k, half):
-        ref = self.out_ref.at[half, lax.rem(self.me + SPOTS - k, SPOTS)]
+        ref = self.out_ref.at[half, self.origin(k)]
         return self.copy(4, k, ref, ref, self.partner)
 
     def merge(self, k):
         self.core_copy(k).wait()
-        j = lax.rem(self.me + k, SPOTS)
+        j = self.there(k)
         return self.in_ref[self.core, j].astype(F32) + self.core_s[k].astype(F32)
 
     def loop(self, first, last, step):
@@ -280,15 +296,13 @@
         lax.fori_loop(first, last, body, 0)
 
     def start_core(self):
-        self.loop(1, SPOTS, lambda k: self.core_copy(k).start())
-        self.core_copy(0).start()
+        for k in FAR_FIRST + [0]:
+            self.core_copy(k).start()
 
     def start_plane(self):
-        def step(k):
+        for k in FAR_FIRST:
             self.part_s[k] = self.merge(k).astype(BF16)
             self.plane_copy(k).start()
-
-        self.loop(1, SPOTS, step)
 
     def start_line(self):
         def add(k, total):
@@ -297,7 +311,8 @@
 
         total = lax.fori_loop(1, SPOTS, add, self.merge(0))
         self.line_s[self.lon] = total.astype(BF16)
-        self.loop(1, self.lons, lambda k: self.line_copy(k, self.lon).start())
+        for k in self.far_line:
+            self.line_copy(k, self.lon).start()
 
     def start_back(self):
         def wait(k):
@@ -309,23 +324,19 @@
         for n in range(1, self.lons):
             total = total + self.line_s[n].astype(F32)
         self.out_ref[self.core, self.me] = total.astype(BF16)
-        self.loop(1, SPOTS, lambda k: self.back_copy(k, self.me).start())
+        for k in FAR_FIRST:
+            self.back_copy(k, self.me).start()
         self.last_copy(0, self.core).start()
 
     def start_last(self):
-        def step(k):
-            self.back_copy(k, self.me).wait_send()
-            self.back_copy(k, lax.rem(self.me + SPOTS - k, SPOTS)).wait_recv()
+        for k in FAR_FIRST[::-1]:
+            self.back_copy(k, self.origin(k)).wait_recv()
             self.last_copy(k, self.core).start()
 
-        self.loop(1, SPOTS, step)
-
     def finish(self):
-        def step(k):
-            self.last_copy(k, self.core).wait_send()
-            self.last_copy(k, 1 - self.core).wait_recv()
-
-        self.loop(0, SPOTS, step)
+        self.loop(1, SPOTS, lambda k: self.back_copy(k, self.me).wait_send())
+        self.loop(0, SPOTS, lambda k: self.last_copy(k, self.core).wait_send())
+        self.loop(0, SPOTS, lambda k: self.last_copy(k, 1 - self.core).wait_recv())
 
 
 def layer_kernel(
@@ -345,6 +356,8 @@
     route_ref,
     dtok_ref,
     sum_ref,
+    inputs_s,
+    input_sem,
     scaled_s,
     room,
     save_a,
@@ -409,6 +422,17 @@
     def arrived(leg, window):
         return recv_s[leg, :, window].reshape(4 * SLOT, C)
 
+    sources = (
+        tok_ref, cot_ref, gain_a, qkv_a, out_a, bias_a, gain_b, qkv_b, out_b, bias_b, route_ref
+    )
+    loads = [
+        pltpu.make_async_copy(source, target, input_sem.at[n])
+        for n, (source, target) in enumerate(zip(sources, inputs_s))
+    ]
+    for n in (10, 0, 2, 3, 4, 5, 1, 6, 7, 8, 9):
+        loads[n].start()
+    tok_ref, cot_ref, gain_a, qkv_a, out_a, bias_a, gain_b, qkv_b, out_b, bias_b, route_ref = inputs_s
+
     sum_a = make_sum(lons, (packed_s.at[0], sum_ref.at[0]) + parts_a)
     sum_b = make_sum(lons, (packed_s.at[1], sum_ref.at[1]) + parts_b)
 
@@ -422,7 +446,11 @@
         spot = lax.broadcasted_iota(jnp.int32, (rows, columns), 0)
         return jnp.where(spot == target, 1.0, 0.0).astype(BF16)
 
+    loads[10].wait()
+    loads[0].wait()
     x_a[...] = nn(one_hot(TOK, 0, TOK), tok_ref[...]).astype(BF16)
+    for n in (2, 3, 4, 5):
+        loads[n].wait()
     scaled_s[0] = bias_a[...] * LOG2E
     slots_s[...] = one_hot(16 * SLOT, 2, TOK)
     for n in range(2):
@@ -444,6 +472,7 @@
         mid_s[2 * w] = middle[:72].astype(BF16)
         mid_s[2 * w + 1] = middle[72:].astype(BF16)
         if w == 0:
+            loads[1].wait()
             cots = nn(slots_s[...], cot_ref[...]).astype(BF16)
             cots = cots.reshape(4, WINDOWS, SLOT, C)
             recv_s[0, 0] = cots[0]
@@ -463,6 +492,8 @@
     back_s[...] = one_hot(4 * SLOT, 6, WT)
     for n in range(2):
         home_s[n] = one_hot(72, 7 + n, 4 * SLOT)
+    for n in (6, 7, 8, 9):
+        loads[n].wait()
     scaled_s[1] = bias_b[...] * LOG2E
 
     def label(shape, axis, level):
@@ -482,13 +513,21 @@
 
     for copy in cot_copies:
         copy.wait()
-    for w in range(WINDOWS):
+    gs = [None] * WINDOWS
+
+    def shifted_forward(w):
         for copy in mids[w]:
             copy.wait()
         x = nn(place_s[...], arrived(1, w)).astype(BF16)
-        g = nn(place_s[...], arrived(0, w)).astype(BF16)
-        window_forward(w, x, gb, wqb, wkb, wvb, scaled_s.at[1], extra_s.at[w // (WINDOWS - 1)], save_b)
-        d_in = window_backward(w, w == 0, g, gb, wqb, wkb, wvb, wob, save_b, grad_b)
+        gs[w] = nn(place_s[...], arrived(0, w)).astype(BF16)
+        extra = extra_s.at[w // (WINDOWS - 1)]
+        window_forward(w, x, gb, wqb, wkb, wvb, scaled_s.at[1], extra, save_b)
+
+    shifted_forward(0)
+    for w in range(WINDOWS):
+        if w + 1 < WINDOWS:
+            shifted_forward(w + 1)
+        d_in = window_backward(w, w == 0, gs[w], gb, wqb, wkb, wvb, wob, save_b, grad_b)
         backs[w] = post(2, w, nn(back_s[...], d_in))
 
     pack(packed_s.at[1], grad_b)
@@ -604,9 +643,11 @@
             jax.ShapeDtypeStruct((TOK, C), BF16),
             jax.ShapeDtypeStruct((2, 2, SPOTS, PIECE, 128), BF16),
         ),
-        in_specs=[pl.BlockSpec(memory_space=pltpu.VMEM)] * 11,
+        in_specs=[pl.BlockSpec(memory_space=pl.ANY)] * 11,
         out_specs=(pl.BlockSpec(memory_space=pltpu.VMEM),) * 2,
         scratch_shapes=[
+            tuple(pltpu.VMEM(arg.shape, arg.dtype) for arg in args),
+            pltpu.SemaphoreType.DMA((11,)),
             pltpu.VMEM((2, HEADS, WT, WT), F32),
             rooms(),
             saves(),

time: 79.7 us -> 70 us (0.88)
  local copies, waits for them, and re-layouts: 10.1 us -> 0 us
    unnamed x22 -> x0, local copies, waits for them, and re-layouts: 10.1 us -> none
    pallas_call x1, Pallas kernels: 1.93 us -> 3.28 us  [run_unpack(): pl.pallas_call(unpack_kernel, out_shape=(jax.ShapeDtypeStruct((TOK, C), B...]
where the time goes in v4:
time: 70 us; the launch traced here: 69.9 us
  Pallas kernels  69.2 us (99%)
    pallas_call x1, Pallas kernels, run_layer(): pl.pallas_call(functools.partial(layer_kernel, lats, lons, Sum), out_shap...  65.9 us
    pallas_call x1, Pallas kernels, run_unpack(): pl.pallas_call(unpack_kernel, out_shape=(jax.ShapeDtypeStruct((TOK, C), B...  3.28 us

profile of v4, /device:TPU:1, one launch (start us, length us, event | category | flops | bytes accessed | tf_op | source)
XLA Modules:
  0.0 69.9 jit_solution(9701449521245616663)
XLA Ops:
  0.6 65.9 %layer.1 = (bf16[576,192]{1,0:T(8,128)(2,1)}, bf16[2,2,16,80,128]{4,3,2,1,0:T(8,128)(2,1)}) custom-call(bf16[576,192]{1,0:T(8,128)(2,1)} %bitcast.15, bf16[576,192]{1,0:T(8,128)(2,1)} %bitcast.16, f32[1,192]{1,0:T(1,128)} %bitcast.17, bf16[192,576]{1,0:T(8,128)(2,1)} %qkv_a.1, bf16[192,192]{1,0:T(8,128)(2,1)} %out_a.1, f32[6,144,144]{2,1,0:T(8,128)} %bias_a.1, ...), custom_call_target="tpu_custom_call" | custom-call | tf_op jit(solution)/shard_map/layer/pallas_call | solution.py:640
  66.6 3.3 %unpack.1 = (bf16[576,192]{1,0:T(8,128)(2,1)}, f32[1,192]{1,0:T(1,128)}, f32[192,576]{1,0:T(8,128)}, f32[192,192]{1,0:T(8,128)}, f32[6,144,144]{2,1,0:T(8,128)},...) custom-call(bf16[5120,128]{1,0:T(8,128)(2,1)} %bitcast.14, ...), custom_call_target="tpu_custom_call" | custom-call | tf_op jit(solution)/shard_map/unpack/pallas_call | solution.py:689

commit v5 on v4

--- a/solution.py
+++ b/solution.py
@@ -324,6 +324,9 @@
         for n in range(1, self.lons):
             total = total + self.line_s[n].astype(F32)
         self.out_ref[self.core, self.me] = total.astype(BF16)
+        self.send_back()
+
+    def send_back(self):
         for k in FAR_FIRST:
             self.back_copy(k, self.me).start()
         self.last_copy(0, self.core).start()
@@ -339,10 +342,112 @@
         self.loop(0, SPOTS, lambda k: self.last_copy(k, 1 - self.core).wait_recv())
 
 
+class RingSum(Sum):
+    ORDER = (2, 1, 3)
+
+    def row(self, step):
+        return lax.rem(self.x + 4 + step, 4)
+
+    def group(self, step):
+        return pl.ds(self.row(step) * 4, 4)
+
+    def x_device(self, step):
+        x = self.row(step)
+        return {"rep": (x // 2) * 2 + self.core, "lat": (x % 2) * 4 + self.y}
+
+    def column(self, step):
+        return lax.rem(self.y + 4 + step, 4)
+
+    def y_device(self, step):
+        return {"lat": (self.x % 2) * 4 + self.column(step)}
+
+    def core_copy(self, dx):
+        part = self.group(dx)
+        source = self.in_ref.at[1 - self.core, part]
+        return self.copy(0, dx, source, self.core_s.at[part], self.partner)
+
+    def x_copy(self, dx):
+        target = self.plane_s.at[pl.ds(4 * dx, 4)]
+        return self.copy(1, dx, self.part_s.at[self.group(dx)], target, self.x_device(dx))
+
+    def y_copy(self, dy):
+        source = self.part_s.at[self.x * 4 + self.column(dy)]
+        return self.copy(1, 4 + dy, source, self.plane_s.at[dy], self.y_device(dy))
+
+    def y_back(self, dy, owner):
+        ref = self.out_ref.at[self.core, self.x * 4 + owner]
+        return self.copy(3, 4 + dy, ref, ref, self.y_device(dy))
+
+    def x_back(self, dx, part):
+        ref = self.out_ref.at[self.core, part]
+        return self.copy(3, dx, ref, ref, self.x_device(dx))
+
+    def last_group(self, dx, half):
+        ref = self.out_ref.at[half, self.group(-dx)]
+        return self.copy(4, dx, ref, ref, self.partner)
+
+    def merge(self, dx):
+        self.core_copy(dx).wait()
+        part = self.group(dx)
+        return self.in_ref[self.core, part].astype(F32) + self.core_s[part].astype(F32)
+
+    def start_core(self):
+        for dx in self.ORDER + (0,):
+            self.core_copy(dx).start()
+
+    def start_plane(self):
+        for dx in self.ORDER:
+            self.part_s[self.group(dx)] = self.merge(dx).astype(BF16)
+            self.x_copy(dx).start()
+
+    def start_second(self):
+        total = self.merge(0)
+        for dx in self.ORDER:
+            self.x_copy(dx).wait()
+            total = total + self.plane_s[4 * dx : 4 * dx + 4].astype(F32)
+        self.part_s[self.group(0)] = total.astype(BF16)
+        for dy in self.ORDER:
+            self.y_copy(dy).start()
+
+    def start_line(self):
+        total = self.part_s[self.me].astype(F32)
+        for dy in self.ORDER:
+            self.y_copy(dy).wait()
+            total = total + self.plane_s[dy].astype(F32)
+        self.line_s[self.lon] = total.astype(BF16)
+        for k in self.far_line:
+            self.line_copy(k, self.lon).start()
+
+    def send_back(self):
+        for dy in self.ORDER:
+            self.y_back(dy, self.y).start()
+
+    def start_back_x(self):
+        for dy in self.ORDER:
+            self.y_back(dy, self.y).wait_send()
+            self.y_back(dy, self.column(-dy)).wait_recv()
+        for dx in self.ORDER:
+            self.x_back(dx, self.group(0)).start()
+        self.last_group(0, self.core).start()
+
+    def start_last(self):
+        for dx in self.ORDER:
+            self.x_back(dx, self.group(-dx)).wait_recv()
+            self.last_group(dx, self.core).start()
+
+    def finish(self):
+        for dx in self.ORDER:
+            self.x_back(dx, self.group(0)).wait_send()
+        for dx in (0,) + self.ORDER:
+            self.last_group(dx, self.core).wait_send()
+            self.last_group(dx, 1 - self.core).wait_recv()
+
+
 def layer_kernel(
     lats,
     lons,
     make_sum,
+    make_ring,
     tok_ref,
     cot_ref,
     gain_a,
@@ -354,8 +459,11 @@
     out_b,
     bias_b,
     route_ref,
-    dtok_ref,
+    dtok_out,
+    sum_out,
+    dtok_s,
     sum_ref,
+    out_sem,
     inputs_s,
     input_sem,
     scaled_s,
@@ -434,7 +542,7 @@
     tok_ref, cot_ref, gain_a, qkv_a, out_a, bias_a, gain_b, qkv_b, out_b, bias_b, route_ref = inputs_s
 
     sum_a = make_sum(lons, (packed_s.at[0], sum_ref.at[0]) + parts_a)
-    sum_b = make_sum(lons, (packed_s.at[1], sum_ref.at[1]) + parts_b)
+    sum_b = make_ring(lons, (packed_s.at[1], sum_ref.at[1]) + parts_b)
 
     barrier = pltpu.get_barrier_semaphore()
     for other in before + after:
@@ -478,14 +586,14 @@
             recv_s[0, 0] = cots[0]
             for n in range(1, 4):
                 send_s[0, n] = cots[n]
-        else:
-            if w == 1:
-                pl.semaphore_wait(barrier, greeted)
-                cot_copies = quarters(0, None)
-                for copy in cot_copies:
-                    copy.start()
-            send_mid(w - 1)
-    send_mid(WINDOWS - 1)
+        if w == 1:
+            pl.semaphore_wait(barrier, greeted)
+            cot_copies = quarters(0, None)
+            for copy in cot_copies:
+                copy.start()
+            send_mid(0)
+    for w in range(1, WINDOWS):
+        send_mid(w)
 
     order_s[...] = one_hot(TOK, 1, TOK)
     place_s[...] = one_hot(WT, 5, 4 * SLOT)
@@ -530,9 +638,6 @@
         d_in = window_backward(w, w == 0, gs[w], gb, wqb, wkb, wvb, wob, save_b, grad_b)
         backs[w] = post(2, w, nn(back_s[...], d_in))
 
-    pack(packed_s.at[1], grad_b)
-    sum_b.start_core()
-
     def take_back(w):
         for copy in backs[w]:
             copy.wait()
@@ -549,31 +654,57 @@
     take_back(0)
     take_back(1)
     regular_back(1, True)
-    sum_b.start_plane()
+    pack(packed_s.at[1], grad_b)
+    sum_b.start_core()
     take_back(2)
     regular_back(2, False)
+    sum_b.start_plane()
     take_back(3)
     regular_back(3, False)
     regular_back(0, False)
     pack(packed_s.at[0], grad_a)
     sum_a.start_core()
-    dtok_ref[...] = nn(order_s[...], x_a[...]).astype(BF16)
     sum_a.start_plane()
+    sum_b.start_second()
+    dtok_s[...] = nn(order_s[...], x_a[...]).astype(BF16)
+    leave = [
+        pltpu.make_async_copy(dtok_s, dtok_out, out_sem.at[0]),
+        pltpu.make_async_copy(sum_ref.at[1], sum_out.at[1], out_sem.at[1]),
+        pltpu.make_async_copy(sum_ref.at[0], sum_out.at[0], out_sem.at[2]),
+    ]
+    leave[0].start()
     sum_b.start_line()
+    sum_a.start_line()
     sum_b.start_back()
-    sum_a.start_line()
+    sum_a.start_back()
+    sum_b.start_back_x()
+    sum_a.start_last()
     sum_b.start_last()
-    sum_a.start_back()
-    sum_a.start_last()
     sum_b.finish()
+    leave[1].start()
     sum_a.finish()
-
-
-def unpack_kernel(in_ref, dtok_ref, dtok_out, *outs):
-    dtok_out[...] = dtok_ref[...]
+    leave[2].start()
+    for copy in leave:
+        copy.wait()
+
+
+def unpack_kernel(in_hbm, dtok_ref, dtok_out, *refs):
+    outs, (in_ref, in_sem, held, out_sem) = refs[:8], refs[8:]
+    across = pltpu.make_async_copy(dtok_ref, dtok_out, in_sem.at[2])
+    loads = []
     for block in range(2):
-        gain, qkv, out, bias = outs[4 * block : 4 * block + 4]
+        part = pl.ds(block * 2 * HALF, 2 * HALF)
+        loads.append(pltpu.make_async_copy(in_hbm.at[part], in_ref.at[part], in_sem.at[block]))
+        loads[block].start()
+    across.start()
+    stores = [
+        pltpu.make_async_copy(source, target, out_sem.at[n])
+        for n, (source, target) in enumerate(zip(held, outs))
+    ]
+    for block in range(2):
+        gain, qkv, out, bias = held[4 * block : 4 * block + 4]
         at = block * 2 * HALF
+        loads[block].wait()
 
         def rows(count):
             nonlocal at
@@ -585,13 +716,20 @@
         qkv[...] = jnp.concatenate(
             [gq, one[:, :64], gk, one[:, 64:], gv, two[:, :64]], axis=1
         )
+        stores[4 * block + 1].start()
         out[...] = jnp.concatenate([go, two[:, 64:]], axis=1)
+        stores[4 * block + 2].start()
         main = [rows(WT) for _ in range(HEADS)]
         tails = rows(WT)
         for h in range(HEADS):
             bias[h] = jnp.concatenate([main[h], tails[:, 16 * h : 16 * h + 16]], axis=1)
+        stores[4 * block + 3].start()
         last = rows(16)
         gain[...] = jnp.concatenate([last[0:1, :], last[1:2, :64]], axis=1)
+        stores[4 * block].start()
+    across.wait()
+    for copy in stores:
+        copy.wait()
 
 
 def saves():
@@ -638,14 +776,17 @@
 
 def run_layer(lats, lons, *args):
     return pl.pallas_call(
-        functools.partial(layer_kernel, lats, lons, Sum),
+        functools.partial(layer_kernel, lats, lons, Sum, RingSum),
         out_shape=(
             jax.ShapeDtypeStruct((TOK, C), BF16),
             jax.ShapeDtypeStruct((2, 2, SPOTS, PIECE, 128), BF16),
         ),
         in_specs=[pl.BlockSpec(memory_space=pl.ANY)] * 11,
-        out_specs=(pl.BlockSpec(memory_space=pltpu.VMEM),) * 2,
+        out_specs=(pl.BlockSpec(memory_space=pl.ANY),) * 2,
         scratch_shapes=[
+            pltpu.VMEM((TOK, C), BF16),
+            pltpu.VMEM((2, 2, SPOTS, PIECE, 128), BF16),
+            pltpu.SemaphoreType.DMA((3,)),
             tuple(pltpu.VMEM(arg.shape, arg.dtype) for arg in args),
             pltpu.SemaphoreType.DMA((11,)),
             pltpu.VMEM((2, HEADS, WT, WT), F32),
@@ -689,8 +830,14 @@
     return pl.pallas_call(
         unpack_kernel,
         out_shape=(jax.ShapeDtypeStruct((TOK, C), BF16),) + block + block,
-        in_specs=[pl.BlockSpec(memory_space=pltpu.VMEM)] * 2,
-        out_specs=(pl.BlockSpec(memory_space=pltpu.VMEM),) * 9,
+        in_specs=[pl.BlockSpec(memory_space=pl.ANY)] * 2,
+        out_specs=(pl.BlockSpec(memory_space=pl.ANY),) * 9,
+        scratch_shapes=[
+            pltpu.VMEM((4 * HALF, 128), BF16),
+            pltpu.SemaphoreType.DMA((3,)),
+            tuple(pltpu.VMEM(out.shape, out.dtype) for out in block + block),
+            pltpu.SemaphoreType.DMA((8,)),
+        ],
         compiler_params=pltpu.CompilerParams(vmem_limit_bytes=VMEM_LIMIT),
         name="unpack",
     )(summed, d_tokens)

time: 70 us -> 82.4 us (1.18)
  Pallas kernels: 69.2 us -> 81.5 us
    pallas_call x1, Pallas kernels: 3.28 us -> 10.2 us  [run_unpack(): pl.pallas_call(unpack_kernel, out_shape=(jax.ShapeDtypeStruct((TOK, C), B...]
    pallas_call x1, Pallas kernels: 65.9 us -> 71.3 us  [run_layer(): pl.pallas_call(functools.partial(layer_kernel, lats, lons, Sum, RingSum),...]
where the time goes in v5:
time: 82.4 us; the launch traced here: 82.3 us
  Pallas kernels  81.5 us (99%)
    pallas_call x1, Pallas kernels, run_layer(): pl.pallas_call(functools.partial(layer_kernel, lats, lons, Sum, RingSum),...  71.3 us
    pallas_call x1, Pallas kernels, run_unpack(): pl.pallas_call(unpack_kernel, out_shape=(jax.ShapeDtypeStruct((TOK, C), B...  10.2 us

profile of v5, /device:TPU:1, one launch (start us, length us, event | category | flops | bytes accessed | tf_op | source)
XLA Modules:
  0.0 82.3 jit_solution(6220866386750628974)
XLA Ops:
  0.6 71.3 %layer.1 = (bf16[576,192]{1,0:T(8,128)(2,1)}, bf16[2,2,16,80,128]{4,3,2,1,0:T(8,128)(2,1)}) custom-call(bf16[576,192]{1,0:T(8,128)(2,1)} %bitcast.15, bf16[576,192]{1,0:T(8,128)(2,1)} %bitcast.16, f32[1,192]{1,0:T(1,128)} %bitcast.17, bf16[192,576]{1,0:T(8,128)(2,1)} %qkv_a.1, bf16[192,192]{1,0:T(8,128)(2,1)} %out_a.1, f32[6,144,144]{2,1,0:T(8,128)} %bias_a.1, ...), custom_call_target="tpu_custom_call" | custom-call | tf_op jit(solution)/shard_map/layer/pallas_call | solution.py:778
  72.0 10.2 %unpack.1 = (bf16[576,192]{1,0:T(8,128)(2,1)}, f32[1,192]{1,0:T(1,128)}, f32[192,576]{1,0:T(8,128)}, f32[192,192]{1,0:T(8,128)}, f32[6,144,144]{2,1,0:T(8,128)},...) custom-call(bf16[5120,128]{1,0:T(8,128)(2,1)} %bitcast.14, ...), custom_call_target="tpu_custom_call" | custom-call | tf_op jit(solution)/shard_map/unpack/pallas_call | solution.py:830

commit v6 on v4

--- a/solution.py
+++ b/solution.py
@@ -27,6 +27,7 @@
 LOG2E = 1.4426950408889634
 SLOT = 48
 VMEM_LIMIT = 56 * 1024 * 1024
+UNPACK_LIMIT = 16 * 1024 * 1024
 
 
 def nt(left, right):
@@ -557,8 +558,8 @@
     regular_back(0, False)
     pack(packed_s.at[0], grad_a)
     sum_a.start_core()
+    sum_a.start_plane()
     dtok_ref[...] = nn(order_s[...], x_a[...]).astype(BF16)
-    sum_a.start_plane()
     sum_b.start_line()
     sum_b.start_back()
     sum_a.start_line()
@@ -640,8 +641,8 @@
     return pl.pallas_call(
         functools.partial(layer_kernel, lats, lons, Sum),
         out_shape=(
-            jax.ShapeDtypeStruct((TOK, C), BF16),
-            jax.ShapeDtypeStruct((2, 2, SPOTS, PIECE, 128), BF16),
+            pltpu.VMEM((TOK, C), BF16),
+            pltpu.VMEM((2, 2, SPOTS, PIECE, 128), BF16),
         ),
         in_specs=[pl.BlockSpec(memory_space=pl.ANY)] * 11,
         out_specs=(pl.BlockSpec(memory_space=pltpu.VMEM),) * 2,
@@ -691,7 +692,7 @@
         out_shape=(jax.ShapeDtypeStruct((TOK, C), BF16),) + block + block,
         in_specs=[pl.BlockSpec(memory_space=pltpu.VMEM)] * 2,
         out_specs=(pl.BlockSpec(memory_space=pltpu.VMEM),) * 9,
-        compiler_params=pltpu.CompilerParams(vmem_limit_bytes=VMEM_LIMIT),
+        compiler_params=pltpu.CompilerParams(vmem_limit_bytes=UNPACK_LIMIT),
         name="unpack",
     )(summed, d_tokens)
 

time: 70 us -> 68.1 us (0.973)
  Pallas kernels: 69.2 us -> 67.3 us
    pallas_call x1, Pallas kernels: 3.28 us -> 1.93 us  [run_unpack(): pl.pallas_call(unpack_kernel, out_shape=(jax.ShapeDtypeStruct((TOK, C), B...]
where the time goes in v6:
time: 68.1 us; the launch traced here: 67.9 us
  Pallas kernels  67.3 us (99%)
    pallas_call x1, Pallas kernels, run_layer(): pl.pallas_call(functools.partial(layer_kernel, lats, lons, Sum), out_shap...  65.4 us
    pallas_call x1, Pallas kernels, run_unpack(): pl.pallas_call(unpack_kernel, out_shape=(jax.ShapeDtypeStruct((TOK, C), B...  1.93 us

profile of v6, /device:TPU:1, one launch (start us, length us, event | category | flops | bytes accessed | tf_op | source)
XLA Modules:
  0.0 67.9 jit_solution(18064479170032965912)
XLA Ops:
  0.6 65.4 %layer.1 = (bf16[576,192]{1,0:T(8,128)(2,1)S(1)}, bf16[2,2,16,80,128]{4,3,2,1,0:T(8,128)(2,1)S(1)}) custom-call(bf16[576,192]{1,0:T(8,128)(2,1)} %bitcast.15, bf16[576,192]{1,0:T(8,128)(2,1)} %bitcast.16, f32[1,192]{1,0:T(1,128)} %bitcast.17, bf16[192,576]{1,0:T(8,128)(2,1)} %qkv_a.1, bf16[192,192]{1,0:T(8,128)(2,1)} %out_a.1, f32[6,144,144]{2,1,0:T(8,128)} %bias_a.1, ...), custom_call_target="tpu_custom_call" | custom-call | tf_op jit(solution)/shard_map/layer/pallas_call | solution.py:641
  66.0 1.9 %unpack.1 = (bf16[576,192]{1,0:T(8,128)(2,1)}, f32[1,192]{1,0:T(1,128)}, f32[192,576]{1,0:T(8,128)}, f32[192,192]{1,0:T(8,128)}, f32[6,144,144]{2,1,0:T(8,128)},...) custom-call(bf16[5120,128]{1,0:T(8,128)(2,1)S(1)} %bitcast.14, ...), custom_call_target="tpu_custom_call" | custom-call | tf_op jit(solution)/shard_map/unpack/pallas_call | solution.py:690

commit v7 on v6

--- a/solution.py
+++ b/solution.py
@@ -266,9 +266,13 @@
             device_id_type=MESH,
         )
 
-    def core_copy(self, k):
-        j = self.there(k)
-        return self.copy(0, k, self.in_ref.at[1 - self.core, j], self.core_s.at[k], self.partner)
+    def group(self, dx):
+        return pl.ds(lax.rem(self.x + 4 + dx, 4) * 4, 4)
+
+    def core_copy(self, dx):
+        part = self.group(dx)
+        source = self.in_ref.at[1 - self.core, part]
+        return self.copy(0, dx, source, self.core_s.at[part], self.partner)
 
     def plane_copy(self, k):
         return self.copy(1, k, self.part_s.at[k], self.plane_s.at[k], self.spot(k))
@@ -280,14 +284,13 @@
         ref = self.out_ref.at[self.core, j]
         return self.copy(3, k, ref, ref, self.spot(k))
 
-    def last_copy(self, k, half):
-        ref = self.out_ref.at[half, self.origin(k)]
-        return self.copy(4, k, ref, ref, self.partner)
+    def last_copy(self, dx, half):
+        ref = self.out_ref.at[half, self.group(-dx)]
+        return self.copy(4, dx, ref, ref, self.partner)
 
     def merge(self, k):
-        self.core_copy(k).wait()
         j = self.there(k)
-        return self.in_ref[self.core, j].astype(F32) + self.core_s[k].astype(F32)
+        return self.in_ref[self.core, j].astype(F32) + self.core_s[j].astype(F32)
 
     def loop(self, first, last, step):
         def body(k, carry):
@@ -297,13 +300,17 @@
         lax.fori_loop(first, last, body, 0)
 
     def start_core(self):
-        for k in FAR_FIRST + [0]:
-            self.core_copy(k).start()
+        for dx in (2, 1, 3, 0):
+            self.core_copy(dx).start()
 
     def start_plane(self):
-        for k in FAR_FIRST:
-            self.part_s[k] = self.merge(k).astype(BF16)
-            self.plane_copy(k).start()
+        for dx in (2, 1, 3, 0):
+            self.core_copy(dx).wait()
+            for dy in (2, 1, 3, 0):
+                k = dx * 4 + dy
+                if k:
+                    self.part_s[k] = self.merge(k).astype(BF16)
+                    self.plane_copy(k).start()
 
     def start_line(self):
         def add(k, total):
@@ -327,17 +334,20 @@
         self.out_ref[self.core, self.me] = total.astype(BF16)
         for k in FAR_FIRST:
             self.back_copy(k, self.me).start()
-        self.last_copy(0, self.core).start()
 
     def start_last(self):
-        for k in FAR_FIRST[::-1]:
-            self.back_copy(k, self.origin(k)).wait_recv()
-            self.last_copy(k, self.core).start()
+        for dx in (0, 1, 3, 2):
+            for dy in (0, 1, 3, 2):
+                k = dx * 4 + dy
+                if k:
+                    self.back_copy(k, self.origin(k)).wait_recv()
+            self.last_copy(dx, self.core).start()
 
     def finish(self):
         self.loop(1, SPOTS, lambda k: self.back_copy(k, self.me).wait_send())
-        self.loop(0, SPOTS, lambda k: self.last_copy(k, self.core).wait_send())
-        self.loop(0, SPOTS, lambda k: self.last_copy(k, 1 - self.core).wait_recv())
+        for dx in range(4):
+            self.last_copy(dx, self.core).wait_send()
+            self.last_copy(dx, 1 - self.core).wait_recv()
 
 
 def layer_kernel(

time: 68.1 us -> 67.5 us (level)
  no operation moved by 1% of the time
where the time goes in v7:
time: 67.5 us; the launch traced here: 67.4 us
  Pallas kernels  66.7 us (99%)
    pallas_call x1, Pallas kernels, run_layer(): pl.pallas_call(functools.partial(layer_kernel, lats, lons, Sum), out_shap...  64.8 us
    pallas_call x1, Pallas kernels, run_unpack(): pl.pallas_call(unpack_kernel, out_shape=(jax.ShapeDtypeStruct((TOK, C), B...  1.93 us

profile of v7, /device:TPU:1, one launch (start us, length us, event | category | flops | bytes accessed | tf_op | source)
XLA Modules:
  0.0 67.4 jit_solution(18125404688948096860)
XLA Ops:
  0.6 64.8 %layer.1 = (bf16[576,192]{1,0:T(8,128)(2,1)S(1)}, bf16[2,2,16,80,128]{4,3,2,1,0:T(8,128)(2,1)S(1)}) custom-call(bf16[576,192]{1,0:T(8,128)(2,1)} %bitcast.15, bf16[576,192]{1,0:T(8,128)(2,1)} %bitcast.16, f32[1,192]{1,0:T(1,128)} %bitcast.17, bf16[192,576]{1,0:T(8,128)(2,1)} %qkv_a.1, bf16[192,192]{1,0:T(8,128)(2,1)} %out_a.1, f32[6,144,144]{2,1,0:T(8,128)} %bias_a.1, ...), custom_call_target="tpu_custom_call" | custom-call | tf_op jit(solution)/shard_map/layer/pallas_call | solution.py:651
  65.4 1.9 %unpack.1 = (bf16[576,192]{1,0:T(8,128)(2,1)}, f32[1,192]{1,0:T(1,128)}, f32[192,576]{1,0:T(8,128)}, f32[192,192]{1,0:T(8,128)}, f32[6,144,144]{2,1,0:T(8,128)},...) custom-call(bf16[5120,128]{1,0:T(8,128)(2,1)S(1)} %bitcast.14, ...), custom_call_target="tpu_custom_call" | custom-call | tf_op jit(solution)/shard_map/unpack/pallas_call | solution.py:700

commit v8 on v7

--- a/solution.py
+++ b/solution.py
@@ -571,10 +571,10 @@
     sum_a.start_plane()
     dtok_ref[...] = nn(order_s[...], x_a[...]).astype(BF16)
     sum_b.start_line()
+    sum_a.start_line()
     sum_b.start_back()
-    sum_a.start_line()
+    sum_a.start_back()
     sum_b.start_last()
-    sum_a.start_back()
     sum_a.start_last()
     sum_b.finish()
     sum_a.finish()

time: 67.5 us -> 66.9 us (level)
  no operation moved by 1% of the time
where the time goes in v8:
time: 66.9 us; the launch traced here: 66.8 us
  Pallas kernels  66.1 us (99%)
    pallas_call x1, Pallas kernels, run_layer(): pl.pallas_call(functools.partial(layer_kernel, lats, lons, Sum), out_shap...  64.2 us
    pallas_call x1, Pallas kernels, run_unpack(): pl.pallas_call(unpack_kernel, out_shape=(jax.ShapeDtypeStruct((TOK, C), B...  1.93 us

profile of v8, /device:TPU:1, one launch (start us, length us, event | category | flops | bytes accessed | tf_op | source)
XLA Modules:
  0.0 66.8 jit_solution(10102828658671702855)
XLA Ops:
  0.6 64.2 %layer.1 = (bf16[576,192]{1,0:T(8,128)(2,1)S(1)}, bf16[2,2,16,80,128]{4,3,2,1,0:T(8,128)(2,1)S(1)}) custom-call(bf16[576,192]{1,0:T(8,128)(2,1)} %bitcast.15, bf16[576,192]{1,0:T(8,128)(2,1)} %bitcast.16, f32[1,192]{1,0:T(1,128)} %bitcast.17, bf16[192,576]{1,0:T(8,128)(2,1)} %qkv_a.1, bf16[192,192]{1,0:T(8,128)(2,1)} %out_a.1, f32[6,144,144]{2,1,0:T(8,128)} %bias_a.1, ...), custom_call_target="tpu_custom_call" | custom-call | tf_op jit(solution)/shard_map/layer/pallas_call | solution.py:651
  64.9 1.9 %unpack.1 = (bf16[576,192]{1,0:T(8,128)(2,1)}, f32[1,192]{1,0:T(1,128)}, f32[192,576]{1,0:T(8,128)}, f32[192,192]{1,0:T(8,128)}, f32[6,144,144]{2,1,0:T(8,128)},...) custom-call(bf16[5120,128]{1,0:T(8,128)(2,1)S(1)} %bitcast.14, ...), custom_call_target="tpu_custom_call" | custom-call | tf_op jit(solution)/shard_map/unpack/pallas_call | solution.py:700
